TPU v7x, 128 devices: a whole 4x4x4 slice. The times are simulated.
128 devices in a mesh: seq: 16 (over y_lo, x, core), head: 8 (over z, y_hi).
Axes of the slice: x: 4, y: 4 (y_hi: 2, y_lo: 2; y = y_hi * 2 + y_lo), z: 4, core: 2. Of those that a mesh axis runs over, the one named last changes fastest.
Arguments:
- queries: bfloat16 [12288, 5120], P(('seq', 'head')), may hold values from -18 to 18
- keys: bfloat16 [12288, 5120], P(('seq', 'head')), may hold values from -18 to 18
- values: bfloat16 [12288, 5120], P(('seq', 'head')), may hold values from -6 to 6
- pairs: int32 [32, 4], P('seq'), may hold values from 0 to 31, as said below
- pair_count: int32 [32], P('seq'), may hold values from 3 to 4, as said below
Outputs:
- attended: bfloat16 [12288, 5120], P(('seq', 'head'))
Inputs may be any that keep to these rules, and one draw needn't show every extreme that they name: `pairs`: row g names 4 distinct tiles whose time, height and width coordinates each differ from those of tile g by at most one; its first entry is g itself. `pair_count`: some tile uses all 4 listed tiles.
All inputs are finite; a program needn't handle non-finite values.
Results may differ from a plain program's by a relative error of at most 0.0047.
Values may be sent and summed in bfloat16 or wider, within the bound.
No kernel may reach another device: no remote copies, remote signals or barrier semaphores. Data moves between devices by JAX's collectives and lax.ppermute only.
A program may use at most 256 MiB of HBM per device.

v0:
```python
import math

import jax
import jax.numpy as jnp
from jax import lax
from jax.sharding import PartitionSpec as P

HEAD_DIM = 128
GRID_H = 4
MAXK = 4


def shifted(x, axis, by):
    length = lax.axis_size(axis)
    pairs = [(i, i + by) for i in range(length) if 0 <= i + by < length]
    return lax.ppermute(x, axis, pairs)


def local(queries, keys, values, pairs, pair_count):
    moved_q, moved_k, moved_v = (
        lax.all_to_all(queries, "head", split_axis=1, concat_axis=0, tiled=True),
        lax.all_to_all(keys, "head", split_axis=1, concat_axis=0, tiled=True),
        lax.all_to_all(values, "head", split_axis=1, concat_axis=0, tiled=True),
    )
    slab_len, feat_width = moved_q.shape
    head_count = feat_width // HEAD_DIM
    own_tiles = pairs.shape[0]
    tile_len = slab_len // own_tiles
    score_scale = 1.0 / math.sqrt(HEAD_DIM)
    stacked = jnp.stack([moved_k, moved_v])
    above = shifted(stacked, "seq", 1)
    below = shifted(stacked, "seq", -1)
    column = jnp.concatenate([above, stacked, below], axis=1)
    before = shifted(column, "seq", GRID_H)
    after = shifted(column, "seq", -GRID_H)
    beside_all = jnp.concatenate([before, column, after], axis=1)
    span = 9
    device = lax.axis_index("seq")
    tile_time = pairs // (GRID_H * own_tiles)
    tile_row = pairs // own_tiles % GRID_H
    tile_col = pairs % own_tiles
    step_time = tile_time - device // GRID_H
    step_row = tile_row - device % GRID_H
    local_tiles = ((step_time + 1) * 3 + step_row + 1) * own_tiles + tile_col
    live_slot = jnp.arange(MAXK, dtype=jnp.int32)[None, :] < pair_count[:, None]
    matches = (
        local_tiles[:, :, None] == jnp.arange(span * own_tiles, dtype=jnp.int32)[None, None, :]
    ) & live_slot[:, :, None]
    allowed = jnp.any(matches, axis=1)
    key_mask = jnp.repeat(jnp.repeat(allowed, tile_len, axis=0), tile_len, axis=1)

    def per_head(head_index):
        query_head = lax.dynamic_slice_in_dim(moved_q, head_index * HEAD_DIM, HEAD_DIM, 1)
        key_head = lax.dynamic_slice_in_dim(beside_all[0], head_index * HEAD_DIM, HEAD_DIM, 1)
        value_head = lax.dynamic_slice_in_dim(beside_all[1], head_index * HEAD_DIM, HEAD_DIM, 1)
        scores = (
            lax.dot_general(
                query_head, key_head, (((1,), (1,)), ((), ())), preferred_element_type=jnp.float32
            )
            * score_scale
        )
        peak = jnp.max(jnp.where(key_mask, scores, -jnp.inf), axis=-1, keepdims=True)
        exps = jnp.where(key_mask, jnp.exp(scores - peak), 0.0)
        weight_sum = jnp.sum(exps, axis=-1)
        probs = exps.astype(jnp.bfloat16)
        output = jnp.dot(probs, value_head, preferred_element_type=jnp.float32)
        output = output / weight_sum[:, None]
        return output.astype(jnp.bfloat16)

    per_heads = lax.map(per_head, jnp.arange(head_count, dtype=jnp.int32))
    gathered = jnp.transpose(per_heads, (1, 0, 2)).reshape(slab_len, feat_width)
    return lax.all_to_all(gathered, "head", split_axis=0, concat_axis=1, tiled=True)


def solution(mesh):
    placed = (
        P(("seq", "head"), None),
        P(("seq", "head"), None),
        P(("seq", "head"), None),
        P("seq", None),
        P("seq"),
    )
    return jax.shard_map(
        local, mesh=mesh, in_specs=placed, out_specs=P(("seq", "head"), None), check_vma=False
    )
```

profile of v0, /device:TPU:1, one launch (start us, length us, event | category | flops | bytes accessed | tf_op | source)
XLA Modules:
  0.0 671.1 jit_solution(13305655892786993305)
XLA Ops:
  0.0 2.2 copy.50
  2.2 8.5 %all-to-all-start.1 = ((bf16[96,8,640]{2,0,1:T(8,128)(2,1)}), bf16[96,8,640]{2,0,1:T(8,128)(2,1)S(1)}, u32[]{:S(2)}, u32[]{:S(2)}) async-start(bf16[96,8,640]{2,0,1:T(8,128)(2,1)} %bitcast.51), calls=%async_computation.1 | async-start | bytes 1966080 | tf_op jit(solution)/shard_map/all_to_all | solution.py:22
  12.0 14.0 %all-to-all-done.1 = bf16[96,8,640]{2,0,1:T(8,128)(2,1)S(1)} async-done(((bf16[96,8,640]{2,0,1:T(8,128)(2,1)}), bf16[96,8,640]{2,0,1:T(8,128)(2,1)S(1)}, u32[]{:S(2)}, u32[]{:S(2)}) %all-to-all-start.1) | async-done | bytes 983072 | tf_op jit(solution)/shard_map/all_to_all | solution.py:22
  26.0 19.7 %all_to_all.70 = bf16[96,8,640]{2,0,1:T(8,128)(2,1)S(1)} all-to-all(bf16[96,8,640]{2,0,1:T(8,128)(2,1)S(1)} %bitcast.72), channel_id=1, replica_groups=mesh['seq'=16,'head'=8] {'head'}, dimensions={1} | all-to-all | bytes 1966080 | tf_op jit(solution)/shard_map/all_to_all | solution.py:23
  45.9 4.8 collective-permute-start
  50.8 1.9 collective-permute-start.1
  52.7 19.6 %collective-permute-done = bf16[2,768,640]{2,1,0:T(8,128)(2,1)S(1)} collective-permute-done((bf16[2,768,640]{2,1,0:T(8,128)(2,1)S(1)}, bf16[2,768,640]{2,1,0:T(8,128)(2,1)S(1)}, u32[]{:S(2)}, u32[]{:S(2)}) %collective-permute-start) | collective-permute-done | bytes 1966112 | tf_op jit(solution)/shard_map/ppermute | solution.py:16
  72.3 4.4 collective-permute-done.1
  78.1 9.8 %pad_maximum_fusion = bf16[2,2304,640]{2,1,0:T(8,128)(2,1)} fusion(bf16[2,768,640]{2,1,0:T(8,128)(2,1)S(1)} %collective-permute-done.1, bf16[1,768,640]{2,1,0:T(8,128)(2,1)S(1)} %bitcast.68, bf16[1,768,640]{2,1,0:T(8,128)(2,1)S(1)} %bitcast.65, bf16[2,768,640]{2,1,0:T(8,128)(2,1)S(1)} %collective-permute-done), kind=kLoop, calls=%fused_computation.20 | loop fusion | flops 23592960 | bytes 11796480 | tf_op jit(solution)/shard_map/concatenate | solution.py:33
  87.8 6.8 %collective-permute-start.2 = (bf16[2,2304,640]{2,1,0:T(8,128)(2,1)}, bf16[2,2304,640]{2,1,0:T(8,128)(2,1)}, u32[]{:S(2)}, u32[]{:S(2)}) collective-permute-start(bf16[2,2304,640]{2,1,0:T(8,128)(2,1)} %pad_maximum_fusion), channel_id=1, source_target_pairs={{0,32},{8,40},{16,48},{24,56},{32,64},{40,72},{48,80},{56,88},{64,... | collective-permute-start | bytes 17694728 | tf_op jit(solution)/shard_map/ppermute | solution.py:16
  97.0 3.6 all-to-all-start
  101.1 117.7 %collective-permute-done.2 = bf16[2,2304,640]{2,1,0:T(8,128)(2,1)} collective-permute-done((bf16[2,2304,640]{2,1,0:T(8,128)(2,1)}, bf16[2,2304,640]{2,1,0:T(8,128)(2,1)}, u32[]{:S(2)}, u32[]{:S(2)}) %collective-permute-start.2) | collective-permute-done | bytes 5898272 | tf_op jit(solution)/shard_map/ppermute | solution.py:16
  218.9 5.6 constant_dynamic-update-slice_fusion.4
  224.5 1.5 constant_dynamic-update-slice_fusion.3
  226.0 1.5 constant_dynamic-update-slice_fusion.2
  227.5 1.4 constant_dynamic-update-slice_fusion.1
  228.9 116.9 %collective-permute-done.3 = bf16[2,2304,640]{2,1,0:T(8,128)(2,1)} collective-permute-done((bf16[2,2304,640]{2,1,0:T(8,128)(2,1)}, bf16[2,2304,640]{2,1,0:T(8,128)(2,1)}, u32[]{:S(2)}, u32[]{:S(2)}) %collective-permute-start.3) | collective-permute-done | bytes 5898272 | tf_op jit(solution)/shard_map/ppermute | solution.py:16
  345.8 5.7 constant_dynamic-update-slice_fusion
  351.5 297.2 %while.11 = (s32[]{:T(128)}, bf16[5,768,128]{2,1,0:T(8,128)(2,1)S(1)}, s32[5]{0:T(128)S(1)}, bf16[768,640]{1,0:T(8,128)(2,1)S(1)}, bf16[2,6912,640]{2,1,0:T(8,12...) while((s32[]{:T(128)}, ...), condition=%wide.region_4.5_spmd.clone, body=%wide.region_1.4_spmd.clone.sunk | while | flops 2776496640 | bytes 219840704 | solution.py:70
  352.9 1.4 broadcast_in_dim.57
  354.3 16.0 %copy.53 = pred[768,6912]{1,0:T(32,128)(4,1)} copy(pred[768,6912]{0,1:T(32,128)(4,1)S(1)} %bitcast.63) | data formatting | bytes 10616832 | tf_op jit(solution)/shard_map/reshape | solution.py:50
  370.3 12.1 %fusion.50 = (bf16[1,6912,640]{2,1,0:T(8,128)(2,1)}, bf16[1,6912,640]{2,1,0:T(8,128)(2,1)}) fusion(bf16[2,6912,640]{2,1,0:T(8,128)(2,1)} %get-tuple-element.138), kind=kLoop, calls=%fused_computation.50.clone.1 | loop fusion | bytes 35389440 | tf_op jit(solution)/shard_map/while/body/eval_jaxpr/slice | solution.py:54
  382.3 7.0 %select_reduce_fusion.2 = (f32[768]{0:T(1024)S(1)}, f32[768,6912]{1,0:T(8,128)S(1)}) fusion(pred[768,6912]{1,0:T(32,128)(4,1)} %copy.53, bf16[1,6912,640]{2,1,0:T(8,128)(2,1)} %get-tuple-element.111, s32[]{:T(128)S(6)} %select_n.90, bf16[768,640]{1,0:T(8,128)(2,1)S(1)} %get-tuple-element.137), kind=kOutput, calls=%fused_computation.2.clone.1 | convolution fusion | flops 1374878976 | bytes 28512256 | tf_op jit(solution)/shard_map/while/body/eval_jaxpr/dot_general | solution.py:57
  389.4 10.0 %fusion.51 = f32[768]{0:T(1024)S(1)} fusion(pred[768,6912]{1,0:T(32,128)(4,1)} %copy.53, f32[768,6912]{1,0:T(8,128)S(1)} %get-tuple-element.112, f32[768]{0:T(1024)S(1)} %get-tuple-element.113), kind=kLoop, calls=%fused_computation.3.clone.1 | loop fusion | flops 21232896 | bytes 26548224 | tf_op jit(solution)/shard_map/while/body/eval_jaxpr/reduce_sum | solution.py:64
  399.4 11.7 %fusion.52 = bf16[5,768,128]{2,1,0:T(8,128)(2,1)S(1)} fusion(bf16[5,768,128]{2,1,0:T(8,128)(2,1)S(1)} %get-tuple-element.125, s32[]{:T(128)} %get-tuple-element.124, bf16[1,6912,640]{2,1,0:T(8,128)(2,1)} %get-tuple-element.110, s32[]{:T(128)S(6)} %select_n.90, pred[768,6912]{1,0:T(32,128)(4,1)} %copy.53, f32[768,6912]{1,0:T(8,128)} %copy-done, ...), kind=kOutput, calls=%fused_computation.14.clone.1 | convolution fusion | flops 1380384768 | bytes 28516868 | tf_op jit(solution)/shard_map/while/body/eval_jaxpr/dot_general | solution.py:66
  413.7 16.0 %copy.53 = pred[768,6912]{1,0:T(32,128)(4,1)} copy(pred[768,6912]{0,1:T(32,128)(4,1)S(1)} %bitcast.63) | data formatting | bytes 10616832 | tf_op jit(solution)/shard_map/reshape | solution.py:50
  429.7 12.1 %fusion.50 = (bf16[1,6912,640]{2,1,0:T(8,128)(2,1)}, bf16[1,6912,640]{2,1,0:T(8,128)(2,1)}) fusion(bf16[2,6912,640]{2,1,0:T(8,128)(2,1)} %get-tuple-element.138), kind=kLoop, calls=%fused_computation.50.clone.1 | loop fusion | bytes 35389440 | tf_op jit(solution)/shard_map/while/body/eval_jaxpr/slice | solution.py:54
  441.7 7.0 %select_reduce_fusion.2 = (f32[768]{0:T(1024)S(1)}, f32[768,6912]{1,0:T(8,128)S(1)}) fusion(pred[768,6912]{1,0:T(32,128)(4,1)} %copy.53, bf16[1,6912,640]{2,1,0:T(8,128)(2,1)} %get-tuple-element.111, s32[]{:T(128)S(6)} %select_n.90, bf16[768,640]{1,0:T(8,128)(2,1)S(1)} %get-tuple-element.137), kind=kOutput, calls=%fused_computation.2.clone.1 | convolution fusion | flops 1374878976 | bytes 28512256 | tf_op jit(solution)/shard_map/while/body/eval_jaxpr/dot_general | solution.py:57
  448.8 10.0 %fusion.51 = f32[768]{0:T(1024)S(1)} fusion(pred[768,6912]{1,0:T(32,128)(4,1)} %copy.53, f32[768,6912]{1,0:T(8,128)S(1)} %get-tuple-element.112, f32[768]{0:T(1024)S(1)} %get-tuple-element.113), kind=kLoop, calls=%fused_computation.3.clone.1 | loop fusion | flops 21232896 | bytes 26548224 | tf_op jit(solution)/shard_map/while/body/eval_jaxpr/reduce_sum | solution.py:64
  458.8 11.7 %fusion.52 = bf16[5,768,128]{2,1,0:T(8,128)(2,1)S(1)} fusion(bf16[5,768,128]{2,1,0:T(8,128)(2,1)S(1)} %get-tuple-element.125, s32[]{:T(128)} %get-tuple-element.124, bf16[1,6912,640]{2,1,0:T(8,128)(2,1)} %get-tuple-element.110, s32[]{:T(128)S(6)} %select_n.90, pred[768,6912]{1,0:T(32,128)(4,1)} %copy.53, f32[768,6912]{1,0:T(8,128)} %copy-done, ...), kind=kOutput, calls=%fused_computation.14.clone.1 | convolution fusion | flops 1380384768 | bytes 28516868 | tf_op jit(solution)/shard_map/while/body/eval_jaxpr/dot_general | solution.py:66
  473.1 16.0 %copy.53 = pred[768,6912]{1,0:T(32,128)(4,1)} copy(pred[768,6912]{0,1:T(32,128)(4,1)S(1)} %bitcast.63) | data formatting | bytes 10616832 | tf_op jit(solution)/shard_map/reshape | solution.py:50
  489.1 12.1 %fusion.50 = (bf16[1,6912,640]{2,1,0:T(8,128)(2,1)}, bf16[1,6912,640]{2,1,0:T(8,128)(2,1)}) fusion(bf16[2,6912,640]{2,1,0:T(8,128)(2,1)} %get-tuple-element.138), kind=kLoop, calls=%fused_computation.50.clone.1 | loop fusion | bytes 35389440 | tf_op jit(solution)/shard_map/while/body/eval_jaxpr/slice | solution.py:54
  501.1 7.0 %select_reduce_fusion.2 = (f32[768]{0:T(1024)S(1)}, f32[768,6912]{1,0:T(8,128)S(1)}) fusion(pred[768,6912]{1,0:T(32,128)(4,1)} %copy.53, bf16[1,6912,640]{2,1,0:T(8,128)(2,1)} %get-tuple-element.111, s32[]{:T(128)S(6)} %select_n.90, bf16[768,640]{1,0:T(8,128)(2,1)S(1)} %get-tuple-element.137), kind=kOutput, calls=%fused_computation.2.clone.1 | convolution fusion | flops 1374878976 | bytes 28512256 | tf_op jit(solution)/shard_map/while/body/eval_jaxpr/dot_general | solution.py:57
  508.2 10.0 %fusion.51 = f32[768]{0:T(1024)S(1)} fusion(pred[768,6912]{1,0:T(32,128)(4,1)} %copy.53, f32[768,6912]{1,0:T(8,128)S(1)} %get-tuple-element.112, f32[768]{0:T(1024)S(1)} %get-tuple-element.113), kind=kLoop, calls=%fused_computation.3.clone.1 | loop fusion | flops 21232896 | bytes 26548224 | tf_op jit(solution)/shard_map/while/body/eval_jaxpr/reduce_sum | solution.py:64
  518.2 11.7 %fusion.52 = bf16[5,768,128]{2,1,0:T(8,128)(2,1)S(1)} fusion(bf16[5,768,128]{2,1,0:T(8,128)(2,1)S(1)} %get-tuple-element.125, s32[]{:T(128)} %get-tuple-element.124, bf16[1,6912,640]{2,1,0:T(8,128)(2,1)} %get-tuple-element.110, s32[]{:T(128)S(6)} %select_n.90, pred[768,6912]{1,0:T(32,128)(4,1)} %copy.53, f32[768,6912]{1,0:T(8,128)} %copy-done, ...), kind=kOutput, calls=%fused_computation.14.clone.1 | convolution fusion | flops 1380384768 | bytes 28516868 | tf_op jit(solution)/shard_map/while/body/eval_jaxpr/dot_general | solution.py:66
  531.1 1.4 broadcast_in_dim.57
  532.5 16.0 %copy.53 = pred[768,6912]{1,0:T(32,128)(4,1)} copy(pred[768,6912]{0,1:T(32,128)(4,1)S(1)} %bitcast.63) | data formatting | bytes 10616832 | tf_op jit(solution)/shard_map/reshape | solution.py:50
  548.5 12.1 %fusion.50 = (bf16[1,6912,640]{2,1,0:T(8,128)(2,1)}, bf16[1,6912,640]{2,1,0:T(8,128)(2,1)}) fusion(bf16[2,6912,640]{2,1,0:T(8,128)(2,1)} %get-tuple-element.138), kind=kLoop, calls=%fused_computation.50.clone.1 | loop fusion | bytes 35389440 | tf_op jit(solution)/shard_map/while/body/eval_jaxpr/slice | solution.py:54
  560.6 7.0 %select_reduce_fusion.2 = (f32[768]{0:T(1024)S(1)}, f32[768,6912]{1,0:T(8,128)S(1)}) fusion(pred[768,6912]{1,0:T(32,128)(4,1)} %copy.53, bf16[1,6912,640]{2,1,0:T(8,128)(2,1)} %get-tuple-element.111, s32[]{:T(128)S(6)} %select_n.90, bf16[768,640]{1,0:T(8,128)(2,1)S(1)} %get-tuple-element.137), kind=kOutput, calls=%fused_computation.2.clone.1 | convolution fusion | flops 1374878976 | bytes 28512256 | tf_op jit(solution)/shard_map/while/body/eval_jaxpr/dot_general | solution.py:57
  567.6 10.0 %fusion.51 = f32[768]{0:T(1024)S(1)} fusion(pred[768,6912]{1,0:T(32,128)(4,1)} %copy.53, f32[768,6912]{1,0:T(8,128)S(1)} %get-tuple-element.112, f32[768]{0:T(1024)S(1)} %get-tuple-element.113), kind=kLoop, calls=%fused_computation.3.clone.1 | loop fusion | flops 21232896 | bytes 26548224 | tf_op jit(solution)/shard_map/while/body/eval_jaxpr/reduce_sum | solution.py:64
  577.6 11.7 %fusion.52 = bf16[5,768,128]{2,1,0:T(8,128)(2,1)S(1)} fusion(bf16[5,768,128]{2,1,0:T(8,128)(2,1)S(1)} %get-tuple-element.125, s32[]{:T(128)} %get-tuple-element.124, bf16[1,6912,640]{2,1,0:T(8,128)(2,1)} %get-tuple-element.110, s32[]{:T(128)S(6)} %select_n.90, pred[768,6912]{1,0:T(32,128)(4,1)} %copy.53, f32[768,6912]{1,0:T(8,128)} %copy-done, ...), kind=kOutput, calls=%fused_computation.14.clone.1 | convolution fusion | flops 1380384768 | bytes 28516868 | tf_op jit(solution)/shard_map/while/body/eval_jaxpr/dot_general | solution.py:66
  591.9 16.0 %copy.53 = pred[768,6912]{1,0:T(32,128)(4,1)} copy(pred[768,6912]{0,1:T(32,128)(4,1)S(1)} %bitcast.63) | data formatting | bytes 10616832 | tf_op jit(solution)/shard_map/reshape | solution.py:50
  607.9 12.1 %fusion.50 = (bf16[1,6912,640]{2,1,0:T(8,128)(2,1)}, bf16[1,6912,640]{2,1,0:T(8,128)(2,1)}) fusion(bf16[2,6912,640]{2,1,0:T(8,128)(2,1)} %get-tuple-element.138), kind=kLoop, calls=%fused_computation.50.clone.1 | loop fusion | bytes 35389440 | tf_op jit(solution)/shard_map/while/body/eval_jaxpr/slice | solution.py:54
  620.0 7.0 %select_reduce_fusion.2 = (f32[768]{0:T(1024)S(1)}, f32[768,6912]{1,0:T(8,128)S(1)}) fusion(pred[768,6912]{1,0:T(32,128)(4,1)} %copy.53, bf16[1,6912,640]{2,1,0:T(8,128)(2,1)} %get-tuple-element.111, s32[]{:T(128)S(6)} %select_n.90, bf16[768,640]{1,0:T(8,128)(2,1)S(1)} %get-tuple-element.137), kind=kOutput, calls=%fused_computation.2.clone.1 | convolution fusion | flops 1374878976 | bytes 28512256 | tf_op jit(solution)/shard_map/while/body/eval_jaxpr/dot_general | solution.py:57
  627.0 10.0 %fusion.51 = f32[768]{0:T(1024)S(1)} fusion(pred[768,6912]{1,0:T(32,128)(4,1)} %copy.53, f32[768,6912]{1,0:T(8,128)S(1)} %get-tuple-element.112, f32[768]{0:T(1024)S(1)} %get-tuple-element.113), kind=kLoop, calls=%fused_computation.3.clone.1 | loop fusion | flops 21232896 | bytes 26548224 | tf_op jit(solution)/shard_map/while/body/eval_jaxpr/reduce_sum | solution.py:64
  637.0 11.7 %fusion.52 = bf16[5,768,128]{2,1,0:T(8,128)(2,1)S(1)} fusion(bf16[5,768,128]{2,1,0:T(8,128)(2,1)S(1)} %get-tuple-element.125, s32[]{:T(128)} %get-tuple-element.124, bf16[1,6912,640]{2,1,0:T(8,128)(2,1)} %get-tuple-element.110, s32[]{:T(128)S(6)} %select_n.90, pred[768,6912]{1,0:T(32,128)(4,1)} %copy.53, f32[768,6912]{1,0:T(8,128)} %copy-done, ...), kind=kOutput, calls=%fused_computation.14.clone.1 | convolution fusion | flops 1380384768 | bytes 28516868 | tf_op jit(solution)/shard_map/while/body/eval_jaxpr/dot_general | solution.py:66
  649.6 1.9 copy.39
  652.7 17.3 %all_to_all.71 = bf16[8,96,640]{2,1,0:T(8,128)(2,1)S(1)} all-to-all(bf16[8,96,640]{2,1,0:T(8,128)(2,1)S(1)} %reshape.56), channel_id=1, replica_groups=mesh['seq'=16,'head'=8] {'head'}, dimensions={0} | all-to-all | bytes 1966080 | tf_op jit(solution)/shard_map/all_to_all | solution.py:72
  (52 shorter events, 15.9 us)
Async XLA Ops:
  2.2 23.8 %all-to-all-start.1 = ((bf16[96,8,640]{2,0,1:T(8,128)(2,1)}), bf16[96,8,640]{2,0,1:T(8,128)(2,1)S(1)}, u32[]{:S(2)}, u32[]{:S(2)}) async-start(bf16[96,8,640]{2,0,1:T(8,128)(2,1)} %bitcast.51), calls=%async_computation.1 | async-start | bytes 1966080 | tf_op jit(solution)/shard_map/all_to_all | solution.py:22
  45.7 50.2 %copy-start.5 = (bf16[96,5120]{1,0:T(8,128)(2,1)S(1)}, bf16[96,5120]{1,0:T(8,128)(2,1)}, u32[]{:S(2)}) copy-start(bf16[96,5120]{1,0:T(8,128)(2,1)} %param.7) | copy-start | bytes 2949124
  45.9 54.7 %copy-start.9 = (s32[2]{0:T(128)S(1)}, s32[2]{0:T(128)}, u32[]{:S(2)}) copy-start(s32[2]{0:T(128)} %param.11) | copy-start | bytes 28
  45.9 54.8 %copy-start.8 = (s32[2,4]{1,0:T(2,128)S(1)}, s32[2,4]{1,0:T(2,128)}, u32[]{:S(2)}) copy-start(s32[2,4]{1,0:T(2,128)} %param.10) | copy-start | bytes 100
  45.9 26.4 %collective-permute-start = (bf16[2,768,640]{2,1,0:T(8,128)(2,1)S(1)}, bf16[2,768,640]{2,1,0:T(8,128)(2,1)S(1)}, u32[]{:S(2)}, u32[]{:S(2)}) collective-permute-start(bf16[2,768,640]{2,1,0:T(8,128)(2,1)S(1)} %pad_maximum_fusion.1), channel_id=1, source_target_pairs={{0,8},{8,16},{16,24},{24,32},{32,40},{40,48},{48,56},{56,64},{64,7... | collective-permute-start | bytes 5898248 | tf_op jit(solution)/shard_map/ppermute | solution.py:16
  50.8 25.9 %collective-permute-start.1 = (bf16[2,768,640]{2,1,0:T(8,128)(2,1)S(1)}, bf16[2,768,640]{2,1,0:T(8,128)(2,1)S(1)}, u32[]{:S(2)}, u32[]{:S(2)}) collective-permute-start(bf16[2,768,640]{2,1,0:T(8,128)(2,1)S(1)} %pad_maximum_fusion.1), channel_id=1, source_target_pairs={{8,0},{16,8},{24,16},{32,24},{40,32},{48,40},{56,48},{64,56},{72,6... | collective-permute-start | bytes 5898248 | tf_op jit(solution)/shard_map/ppermute | solution.py:16
  72.3 15.5 %copy-start.3 = (bf16[2,768,640]{2,1,0:T(8,128)(2,1)}, bf16[2,768,640]{2,1,0:T(8,128)(2,1)S(1)}, u32[]{:S(2)}) copy-start(bf16[2,768,640]{2,1,0:T(8,128)(2,1)S(1)} %collective-permute-done) | copy-start | bytes 5898244
  76.7 1.3 copy-start.1
  87.8 131.1 %collective-permute-start.2 = (bf16[2,2304,640]{2,1,0:T(8,128)(2,1)}, bf16[2,2304,640]{2,1,0:T(8,128)(2,1)}, u32[]{:S(2)}, u32[]{:S(2)}) collective-permute-start(bf16[2,2304,640]{2,1,0:T(8,128)(2,1)} %pad_maximum_fusion), channel_id=1, source_target_pairs={{0,32},{8,40},{16,48},{24,56},{32,64},{40,72},{48,80},{56,88},{64,... | collective-permute-start | bytes 17694728 | tf_op jit(solution)/shard_map/ppermute | solution.py:16
  94.7 251.1 %collective-permute-start.3 = (bf16[2,2304,640]{2,1,0:T(8,128)(2,1)}, bf16[2,2304,640]{2,1,0:T(8,128)(2,1)}, u32[]{:S(2)}, u32[]{:S(2)}) collective-permute-start(bf16[2,2304,640]{2,1,0:T(8,128)(2,1)} %pad_maximum_fusion), channel_id=1, source_target_pairs={{32,0},{40,8},{48,16},{56,24},{64,32},{72,40},{80,48},{88,56},{96,... | collective-permute-start | bytes 17694728 | tf_op jit(solution)/shard_map/ppermute | solution.py:16
  97.0 254.5 %all-to-all-start = ((bf16[96,8,640]{2,0,1:T(8,128)(2,1)}), bf16[96,8,640]{2,0,1:T(8,128)(2,1)S(1)}, u32[]{:S(2)}, u32[]{:S(2)}) async-start(bf16[96,8,640]{2,0,1:T(8,128)(2,1)} %bitcast.71), calls=%async_computation | async-start | bytes 1966080 | tf_op jit(solution)/shard_map/all_to_all | solution.py:21
  100.9 123.6 %copy-start.4 = (bf16[2,768,640]{2,1,0:T(8,128)(2,1)S(1)}, bf16[2,768,640]{2,1,0:T(8,128)(2,1)}, u32[]{:S(2)}) copy-start(bf16[2,768,640]{2,1,0:T(8,128)(2,1)} %copy-done.3) | copy-start | bytes 5898244
  101.1 126.4 %copy-start.2 = (bf16[2,768,640]{2,1,0:T(8,128)(2,1)S(1)}, bf16[2,768,640]{2,1,0:T(8,128)(2,1)}, u32[]{:S(2)}) copy-start(bf16[2,768,640]{2,1,0:T(8,128)(2,1)} %copy-done.1) | copy-start | bytes 5898244
  227.5 124.0 %copy-start.6 = (bf16[5,768,128]{2,1,0:T(8,128)(2,1)S(1)}, bf16[5,768,128]{2,1,0:T(8,128)(2,1)}, u32[]{:S(2)}) copy-start(bf16[5,768,128]{2,1,0:T(8,128)(2,1)} %custom-call.1) | copy-start | bytes 2949124
  389.4 10.0 %copy-start = (f32[768,6912]{1,0:T(8,128)}, f32[768,6912]{1,0:T(8,128)S(1)}, u32[]{:S(2)}) copy-start(f32[768,6912]{1,0:T(8,128)S(1)} %get-tuple-element.112) | copy-start | bytes 63700996 | tf_op jit(solution)/shard_map/while
  448.8 10.0 %copy-start = (f32[768,6912]{1,0:T(8,128)}, f32[768,6912]{1,0:T(8,128)S(1)}, u32[]{:S(2)}) copy-start(f32[768,6912]{1,0:T(8,128)S(1)} %get-tuple-element.112) | copy-start | bytes 63700996 | tf_op jit(solution)/shard_map/while
  508.2 10.0 %copy-start = (f32[768,6912]{1,0:T(8,128)}, f32[768,6912]{1,0:T(8,128)S(1)}, u32[]{:S(2)}) copy-start(f32[768,6912]{1,0:T(8,128)S(1)} %get-tuple-element.112) | copy-start | bytes 63700996 | tf_op jit(solution)/shard_map/while
  567.6 10.0 %copy-start = (f32[768,6912]{1,0:T(8,128)}, f32[768,6912]{1,0:T(8,128)S(1)}, u32[]{:S(2)}) copy-start(f32[768,6912]{1,0:T(8,128)S(1)} %get-tuple-element.112) | copy-start | bytes 63700996 | tf_op jit(solution)/shard_map/while
  627.0 10.0 %copy-start = (f32[768,6912]{1,0:T(8,128)}, f32[768,6912]{1,0:T(8,128)S(1)}, u32[]{:S(2)}) copy-start(f32[768,6912]{1,0:T(8,128)S(1)} %get-tuple-element.112) | copy-start | bytes 63700996 | tf_op jit(solution)/shard_map/while
  648.7 0.9 copy-start.7
where the time goes:
time: 674 us; the launch traced here: 671 us
  waiting for transfers between devices  273 us (41%)
  local copies, waits for them, and re-layouts  176 us (26%)
  matrix products  93.5 us (14%)
  other arithmetic  61.5 us (9%)
  blocking collectives  37 us (5%)
  starting transfers between devices  26.9 us (4%)
    ppermute x4, waiting for transfers between devices, shifted(): return lax.ppermute(x, axis, pairs)  259 us
    reshape x5, local copies, waits for them, and re-layouts, local(): jnp.repeat(jnp.repeat(allowed, tile_len, axis=0), tile_len, axis=1)  79.9 us
    slice x5, local copies, waits for them, and re-layouts, per_head(): beside_all[0]  60.4 us
    dot_general x5, matrix products, per_head(): output = jnp.dot(probs, value_head, preferred_element_type=jnp.float32)  58.3 us
    reduce_sum x5, other arithmetic, per_head(): weight_sum = jnp.sum(exps, axis=-1)  49.8 us
    dot_general x5, matrix products, per_head(): lax.dot_general(query_head, key_head, (((1,), (1,)), ((), ())), preferred...  35.2 us
    all_to_all x1, blocking collectives, local(): lax.all_to_all(values, 'head', split_axis=1, concat_axis=0, tiled=True)  19.7 us
    all_to_all x1, blocking collectives, local(): lax.all_to_all(gathered, 'head', split_axis=0, concat_axis=1, tiled=True)  17.3 us
  transfers between devices with their start and end apart: 6, of which 5 were waited for; matrix products, arithmetic and copies ran while one was open for 3% of the time, Pallas kernels for 0%

commit v1 on v0

v1 whole, which is shorter than its diff:
```python
import functools
import math

import jax
import jax.numpy as jnp
from jax import lax
from jax.experimental import pallas as pl
from jax.experimental.pallas import tpu as pltpu
from jax.sharding import PartitionSpec as P

HEAD_DIM = 128
MAXK = 4
CORES = 2
MIB = 1 << 20


def pack_kernel(q_ref, k_ref, v_ref, o_ref):
    half = q_ref.shape[0] // CORES
    heads = q_ref.shape[1] // HEAD_DIM
    for core in range(CORES):
        rows = pl.ds(core * half, half)
        for h in range(heads):
            cols = pl.ds(h * HEAD_DIM, HEAD_DIM)
            for part, ref in enumerate((k_ref, v_ref, q_ref)):
                o_ref[core * heads + h, pl.ds(part * half, half), :] = ref[rows, cols]


def unpack_kernel(i_ref, o_ref):
    half = i_ref.shape[1]
    heads = i_ref.shape[0] // CORES
    for core in range(CORES):
        for h in range(heads):
            o_ref[pl.ds(core * half, half), pl.ds(h * HEAD_DIM, HEAD_DIM)] = i_ref[core * heads + h]


def attend_kernel(pairs_ref, own_ref, sib_ref, o_ref, *, sources, half):
    g = pl.program_id(0)
    tile_half = sources * half
    factor = math.log2(math.e) / math.sqrt(HEAD_DIM)

    def rows(ref, tile, part):
        block = ref[pl.ds(tile * sources, sources), pl.ds(part * half, half), :]
        return block.reshape(tile_half, HEAD_DIM)

    def body(count):
        query = rows(own_ref, g, 2)
        scores = []
        for m in range(count):
            tile = pairs_ref[g, m]
            key = jnp.concatenate([rows(own_ref, tile, 0), rows(sib_ref, tile, 0)], axis=0)
            scores.append(
                lax.dot_general(
                    query, key, (((1,), (1,)), ((), ())), preferred_element_type=jnp.float32
                )
            )
        peak = functools.reduce(jnp.maximum, [jnp.max(s, axis=-1, keepdims=True) for s in scores])
        total = jnp.zeros((tile_half, 1), jnp.float32)
        out = jnp.zeros((tile_half, HEAD_DIM), jnp.float32)
        for m in range(count):
            tile = pairs_ref[g, m]
            value = jnp.concatenate([rows(own_ref, tile, 1), rows(sib_ref, tile, 1)], axis=0)
            exps = jnp.exp2((scores[m] - peak) * factor)
            total = total + jnp.sum(exps, axis=-1, keepdims=True)
            out = out + jnp.dot(
                exps.astype(jnp.bfloat16), value, preferred_element_type=jnp.float32
            )
        out = (out / total).astype(o_ref.dtype)
        o_ref[...] = out.reshape(sources, half, HEAD_DIM)

    full = pairs_ref[g, MAXK] > MAXK - 1

    @pl.when(full)
    def _():
        body(MAXK)

    @pl.when(jnp.logical_not(full))
    def _():
        body(MAXK - 1)


def local(queries, keys, values, pairs, pair_count):
    axes = ("seq", "head")
    devices = lax.axis_size("seq") * lax.axis_size("head")
    head_size = lax.axis_size("head")
    tokens, width = queries.shape
    half = tokens // CORES
    heads = width // HEAD_DIM
    chips_used = heads // head_size
    group = CORES * head_size
    own_tiles = pairs.shape[0]
    tiles = own_tiles * lax.axis_size("seq")
    sources = devices // tiles

    table = jnp.concatenate([pairs, pair_count[:, None]], axis=1)
    table = lax.all_gather(table, "seq", axis=0, tiled=True)

    packed = pl.pallas_call(
        pack_kernel,
        grid=(chips_used,),
        in_specs=[pl.BlockSpec((tokens, head_size * HEAD_DIM), lambda i: (0, i))] * 3,
        out_specs=pl.BlockSpec((group, 3 * half, HEAD_DIM), lambda i: (i, 0, 0)),
        out_shape=jax.ShapeDtypeStruct((devices, 3 * half, HEAD_DIM), jnp.bfloat16),
        name="pack",
    )(queries, keys, values)
    own = lax.all_to_all(packed, axes, split_axis=0, concat_axis=0, tiled=True)
    swap = [(i, i ^ 1) for i in range(lax.axis_size("seq"))]
    sib = lax.ppermute(own, "seq", swap)

    flops = 4 * tiles * sources * half * MAXK * sources * tokens * HEAD_DIM
    whole = pl.BlockSpec((devices, 3 * half, HEAD_DIM), lambda g, table: (0, 0, 0))
    attended = pl.pallas_call(
        functools.partial(attend_kernel, sources=sources, half=half),
        grid_spec=pltpu.PrefetchScalarGridSpec(
            num_scalar_prefetch=1,
            grid=(tiles,),
            in_specs=[whole, whole],
            out_specs=pl.BlockSpec((sources, half, HEAD_DIM), lambda g, table: (g, 0, 0)),
        ),
        out_shape=jax.ShapeDtypeStruct((devices, half, HEAD_DIM), jnp.bfloat16),
        compiler_params=pltpu.CompilerParams(vmem_limit_bytes=56 * MIB),
        cost_estimate=pl.CostEstimate(
            flops=flops, bytes_accessed=12 * MIB, transcendentals=flops // (4 * HEAD_DIM)
        ),
        name="attend",
    )(table, own, sib)

    back = lax.all_to_all(attended, axes, split_axis=0, concat_axis=0, tiled=True)
    return pl.pallas_call(
        unpack_kernel,
        grid=(chips_used,),
        in_specs=[pl.BlockSpec((group, half, HEAD_DIM), lambda i: (i, 0, 0))],
        out_specs=pl.BlockSpec((tokens, head_size * HEAD_DIM), lambda i: (0, i)),
        out_shape=jax.ShapeDtypeStruct((tokens, width), jnp.bfloat16),
        name="unpack",
    )(back)


def solution(mesh):
    placed = (
        P(("seq", "head"), None),
        P(("seq", "head"), None),
        P(("seq", "head"), None),
        P("seq", None),
        P("seq"),
    )
    return jax.shard_map(
        local, mesh=mesh, in_specs=placed, out_specs=P(("seq", "head"), None), check_vma=False
    )
```

time: 674 us -> 156 us (0.23)
  waiting for transfers between devices: 273 us -> 0.01 us
  local copies, waits for them, and re-layouts: 176 us -> 0.1 us
  matrix products: 93.5 us -> 0 us
  blocking collectives: 37 us -> 118 us
  other arithmetic: 61.5 us -> 0.07 us
  Pallas kernels: 0 us -> 36.6 us
  starting transfers between devices: 26.9 us -> 0.31 us
    ppermute x4 -> x1, waiting for transfers between devices: 259 us -> 0.01 us  [local(): sib = lax.ppermute(own, 'seq', swap)]
    dot_general x10 -> x0, matrix products: 93.5 us -> none  [the longest x5 58.3 us: per_head(): output = jnp.dot(probs, value_head, preferred_element_type=jnp.float32)]
    reshape x5 -> x0, local copies, waits for them, and re-layouts: 79.9 us -> none  [local(): jnp.repeat(jnp.repeat(allowed, tile_len, axis=0), tile_len, axis=1)]
    all_to_all x2, blocking collectives: 37 us -> 98.6 us  [the longest x1 70.6 us: local(): own = lax.all_to_all(packed, axes, split_axis=0, concat_axis=0, tiled=True)]
    slice x5 -> x0, local copies, waits for them, and re-layouts: 60.4 us -> none  [per_head(): beside_all[0]]
    reduce_sum x5 -> x0, other arithmetic: 49.8 us -> none  [per_head(): weight_sum = jnp.sum(exps, axis=-1)]
    pallas_call x0 -> x3, Pallas kernels: none -> 36.6 us  [the longest x1 27.6 us: local(): pl.pallas_call(functools.partial(attend_kernel, sources=sources, half=hal...]
    all_gather x0 -> x1, blocking collectives: none -> 19.5 us  [local(): table = lax.all_gather(table, 'seq', axis=0, tiled=True)]
  transfers between devices with their start and end apart: 6 -> 1, of which waited for: 5 -> 0; matrix products, arithmetic and copies ran while one was open for 3% -> 0% of each run, Pallas kernels for 0% -> 0%
where the time goes in v1:
time: 156 us; the launch traced here: 155 us
  blocking collectives  118 us (76%)
  Pallas kernels  36.6 us (23%)
    all_to_all x1, blocking collectives, local(): own = lax.all_to_all(packed, axes, split_axis=0, concat_axis=0, tiled=True)  70.6 us
    all_to_all x1, blocking collectives, local(): lax.all_to_all(attended, axes, split_axis=0, concat_axis=0, tiled=True)  28 us
    pallas_call x1, Pallas kernels, local(): pl.pallas_call(functools.partial(attend_kernel, sources=sources, half=hal...  27.6 us
    all_gather x1, blocking collectives, local(): table = lax.all_gather(table, 'seq', axis=0, tiled=True)  19.5 us
    pallas_call x1, Pallas kernels, local(): pl.pallas_call(pack_kernel, grid=(chips_used,), in_specs=[pl.BlockSpec((t...  5.16 us
    pallas_call x1, Pallas kernels, local(): pl.pallas_call(unpack_kernel, grid=(chips_used,), in_specs=[pl.BlockSpec(...  3.83 us
  transfers between devices with their start and end apart: 1, of which 0 were waited for; matrix products, arithmetic and copies ran while one was open for 0% of the time, Pallas kernels for 0%

profile of v1, /device:TPU:1, one launch (start us, length us, event | category | flops | bytes accessed | tf_op | source)
XLA Modules:
  0.0 155.1 jit_solution(7974372610938280700)
XLA Ops:
  0.0 5.2 %pack.1 = bf16[128,144,128]{2,1,0:T(8,128)(2,1)} custom-call(bf16[96,5120]{1,0:T(8,128)(2,1)} %q_ref.1, bf16[96,5120]{1,0:T(8,128)(2,1)} %k_ref.1, bf16[96,5120]{1,0:T(8,128)(2,1)} %v_ref.1), custom_call_target="tpu_custom_call" | custom-call | tf_op jit(solution)/shard_map/pack/pallas_call | solution.py:97
  5.2 0.0 copy-start.1
  5.2 0.0 copy-start
  5.2 70.6 %all_to_all.10.own_ref = bf16[128,144,128]{2,1,0:T(8,128)(2,1)} all-to-all(bf16[128,144,128]{2,1,0:T(8,128)(2,1)} %pack.1), channel_id=1, replica_groups=mesh['seq'=16,'head'=8] {'seq','head'}, dimensions={0} | all-to-all | bytes 9437184 | tf_op jit(solution)/shard_map/all_to_all | solution.py:105
  75.8 0.3 collective-permute-start
  76.1 0.0 copy-done.1
  76.1 0.1 copy.7
  76.2 0.0 copy-done
  76.2 0.1 add_bitcast_fusion
  76.3 19.5 %all-gather = s32[16,2,5]{2,1,0:T(2,128)} all-gather(s32[1,2,5]{2,1,0:T(2,128)S(1)} %add_bitcast_fusion), channel_id=1, replica_groups=mesh['seq'=16,'head'=8] {'seq'}, dimensions={0}, use_global_device_ids=true | all-gather | bytes 680 | tf_op jit(solution)/shard_map/all_gather | solution.py:95
  95.7 0.0 collective-permute-done.sib_ref
  95.7 27.6 %attend.1 = bf16[128,48,128]{2,1,0:T(8,128)(2,1)} custom-call(s32[32,5]{1,0:T(8,128)} %bitcast.4, bf16[128,144,128]{2,1,0:T(8,128)(2,1)} %all_to_all.10.own_ref, bf16[128,144,128]{2,1,0:T(8,128)(2,1)} %collective-permute-done.sib_ref), custom_call_target="tpu_custom_call" | custom-call | flops 4831838208 | bytes 12582912 | tf_op jit(solution)/shard_map/attend/pallas_call | solution.py:111
  123.3 28.0 %all_to_all.11.i_ref = bf16[128,48,128]{2,1,0:T(8,128)(2,1)} all-to-all(bf16[128,48,128]{2,1,0:T(8,128)(2,1)} %attend.1), channel_id=1, replica_groups=mesh['seq'=16,'head'=8] {'seq','head'}, dimensions={0} | all-to-all | bytes 3145728 | tf_op jit(solution)/shard_map/all_to_all | solution.py:127
  151.3 3.8 %unpack.1 = bf16[96,5120]{1,0:T(8,128)(2,1)} custom-call(bf16[128,48,128]{2,1,0:T(8,128)(2,1)} %all_to_all.11.i_ref), custom_call_target="tpu_custom_call" | custom-call | tf_op jit(solution)/shard_map/unpack/pallas_call | solution.py:128
Async XLA Ops:
  5.2 70.9 %copy-start.1 = (s32[2]{0:T(128)S(1)}, s32[2]{0:T(128)}, u32[]{:S(2)}) copy-start(s32[2]{0:T(128)} %param.9) | copy-start | bytes 28
  5.2 71.0 %copy-start = (s32[2,4]{1,0:T(2,128)S(1)}, s32[2,4]{1,0:T(2,128)}, u32[]{:S(2)}) copy-start(s32[2,4]{1,0:T(2,128)} %param.8) | copy-start | bytes 100
  75.8 19.9 %collective-permute-start = (bf16[128,144,128]{2,1,0:T(8,128)(2,1)}, bf16[128,144,128]{2,1,0:T(8,128)(2,1)}, u32[]{:S(2)}, u32[]{:S(2)}) collective-permute-start(bf16[128,144,128]{2,1,0:T(8,128)(2,1)} %all_to_all.10.own_ref), channel_id=1, source_target_pairs={{0,8},{8,0},{16,24},{24,16},{32,40},{40,32},{48,56},{56,48},{64,72... | collective-permute-start | bytes 14155784 | tf_op jit(solution)/shard_map/ppermute | solution.py:107

commit v2 on v1

v2 whole, which is shorter than its diff:
```python
import functools
import math

import jax
import jax.numpy as jnp
from jax import lax
from jax.experimental import pallas as pl
from jax.experimental.pallas import tpu as pltpu
from jax.sharding import PartitionSpec as P

HEAD_DIM = 128
GRID_H = 4
MAXK = 4
CORES = 2
UNROLL = 2
MIB = 1 << 20


def pack_kernel(q_ref, k_ref, v_ref, o_ref):
    half = q_ref.shape[0] // CORES
    heads = q_ref.shape[1] // HEAD_DIM
    for core in range(CORES):
        rows = pl.ds(core * half, half)
        for h in range(heads):
            cols = pl.ds(h * HEAD_DIM, HEAD_DIM)
            for part, ref in enumerate((k_ref, v_ref, q_ref)):
                o_ref[core * heads + h, pl.ds(part * half, half), :] = ref[rows, cols]


def unpack_kernel(i_ref, o_ref):
    half = i_ref.shape[1]
    heads = i_ref.shape[0] // CORES
    for core in range(CORES):
        for h in range(heads):
            o_ref[pl.ds(core * half, half), pl.ds(h * HEAD_DIM, HEAD_DIM)] = i_ref[core * heads + h]


def attend_kernel(*refs, sources, half, slabs):
    where, parts = refs[0], refs[1 : 1 + slabs]
    own_hbm, sib_hbm, o_ref, own, sib, table, order, sems = refs[1 + slabs :]
    tile_half = sources * half
    tiles = own.shape[0] // sources
    slab_len = own.shape[0] // slabs
    slab_tiles = tiles // slabs
    row_tiles = slab_tiles // GRID_H
    factor = math.log2(math.e) / math.sqrt(HEAD_DIM)

    def copies(slab):
        at = pl.ds(slab * slab_len, slab_len)
        return (
            pltpu.make_async_copy(own_hbm.at[at], own.at[at], sems.at[0, slab]),
            pltpu.make_async_copy(
                sib_hbm.at[at, pl.ds(0, 2 * half)], sib.at[at], sems.at[1, slab]
            ),
        )

    for slab in range(slabs):
        for copy in copies(slab):
            copy.start()

    my_slab, my_row = where[0] // GRID_H, where[0] % GRID_H
    for e in range(slabs):
        for d in range(GRID_H):
            row = (my_slab + slabs - e) % slabs * GRID_H + (my_row + GRID_H - d) % GRID_H
            for w in range(row_tiles):
                for m in range(MAXK):
                    table[row * row_tiles + w, m] = parts[e][d, w * MAXK + m]
                table[row * row_tiles + w, MAXK] = parts[e][d, row_tiles * MAXK + w]

    def sort(g, filled):
        full = table[g, MAXK] > MAXK - 1
        n_full, n_less = filled

        @pl.when(full)
        def _():
            order[0, n_full] = g

        @pl.when(jnp.logical_not(full))
        def _():
            order[1, n_less] = g

        step = full.astype(jnp.int32)
        return n_full + step, n_less + 1 - step

    filled = lax.fori_loop(0, tiles, sort, (jnp.int32(0), jnp.int32(0)))

    def rows(ref, tile, part):
        block = ref[pl.ds(tile * sources, sources), pl.ds(part * half, half), :]
        return block.reshape(tile_half, HEAD_DIM)

    def both(tile, part):
        return jnp.concatenate([rows(own, tile, part), rows(sib, tile, part)], axis=0)

    def attend(g, count):
        query = rows(own, g, 2)
        scores = [
            lax.dot_general(
                query,
                both(table[g, m], 0),
                (((1,), (1,)), ((), ())),
                preferred_element_type=jnp.float32,
            )
            for m in range(count)
        ]
        peak = jnp.max(functools.reduce(jnp.maximum, scores), axis=-1, keepdims=True)
        out = jnp.zeros((tile_half, 2 * HEAD_DIM), jnp.float32)
        for m in range(count):
            probs = jnp.exp2((scores[m] - peak) * factor).astype(jnp.bfloat16)
            value = both(table[g, m], 1)
            value = jnp.concatenate([value, jnp.ones_like(value)], axis=1)
            out = out + jnp.dot(probs, value, preferred_element_type=jnp.float32)
        return out[:, :HEAD_DIM] / out[:, HEAD_DIM:]

    def loaded(have, need):
        for slab in range(slabs):

            @pl.when(jnp.logical_and(have <= slab, slab < need))
            def _(slab=slab):
                for copy in copies(slab):
                    copy.wait()

        return jnp.maximum(have, need)

    have = jnp.int32(0)
    for kind, count in enumerate((MAXK, MAXK - 1)):
        number = filled[kind]

        def step(i, have, kind=kind, count=count, number=number):
            picked = [
                order[kind, jnp.minimum(i * UNROLL + u, number - 1)] for u in range(UNROLL)
            ]
            have = loaded(have, jnp.minimum(picked[-1] // slab_tiles + 2, slabs))
            outs = [attend(g, count) for g in picked]
            for g, out in zip(picked, outs):
                o_ref[pl.ds(g * sources, sources)] = out.astype(o_ref.dtype).reshape(
                    sources, half, HEAD_DIM
                )
            return have

        have = lax.fori_loop(0, (number + UNROLL - 1) // UNROLL, step, have)
    loaded(have, slabs)


def local(queries, keys, values, pairs, pair_count):
    axes = ("seq", "head")
    rows_all = lax.axis_size("seq")
    devices = rows_all * lax.axis_size("head")
    head_size = lax.axis_size("head")
    tokens, width = queries.shape
    half = tokens // CORES
    heads = width // HEAD_DIM
    chips_used = heads // head_size
    group = CORES * head_size
    own_tiles = pairs.shape[0]
    tiles = own_tiles * rows_all
    sources = devices // tiles
    slabs = rows_all // GRID_H

    entry = jnp.concatenate([pairs.reshape(1, -1), pair_count.reshape(1, -1)], axis=1)
    in_slab = [entry] + [
        lax.ppermute(
            entry,
            "seq",
            [(s, s // GRID_H * GRID_H + (s + d) % GRID_H) for s in range(rows_all)],
        )
        for d in range(1, GRID_H)
    ]
    in_slab = jnp.concatenate(in_slab, axis=0)

    packed = pl.pallas_call(
        pack_kernel,
        grid=(chips_used,),
        in_specs=[pl.BlockSpec((tokens, head_size * HEAD_DIM), lambda i: (0, i))] * 3,
        out_specs=pl.BlockSpec((group, 3 * half, HEAD_DIM), lambda i: (i, 0, 0)),
        out_shape=jax.ShapeDtypeStruct((devices, 3 * half, HEAD_DIM), jnp.bfloat16),
        name="pack",
    )(queries, keys, values)
    own = lax.all_to_all(packed, axes, split_axis=0, concat_axis=0, tiled=True)
    sib = lax.ppermute(own, "seq", [(s, s ^ 1) for s in range(rows_all)])
    in_slab, own = lax.optimization_barrier((in_slab, own))
    parts = [in_slab] + [
        lax.ppermute(in_slab, "seq", [(s, (s + e * GRID_H) % rows_all) for s in range(rows_all)])
        for e in range(1, slabs)
    ]
    where = lax.axis_index("seq").astype(jnp.int32).reshape(1)

    flops = 4 * tiles * sources * half * MAXK * sources * tokens * HEAD_DIM
    anywhere = pl.BlockSpec(memory_space=pl.ANY)
    attended = pl.pallas_call(
        functools.partial(attend_kernel, sources=sources, half=half, slabs=slabs),
        grid_spec=pltpu.PrefetchScalarGridSpec(
            num_scalar_prefetch=1 + slabs,
            grid=(1,),
            in_specs=[anywhere, anywhere],
            out_specs=pl.BlockSpec((devices, half, HEAD_DIM), lambda i, *_: (0, 0, 0)),
            scratch_shapes=[
                pltpu.VMEM((devices, 3 * half, HEAD_DIM), jnp.bfloat16),
                pltpu.VMEM((devices, 2 * half, HEAD_DIM), jnp.bfloat16),
                pltpu.SMEM((tiles, MAXK + 1), jnp.int32),
                pltpu.SMEM((2, tiles), jnp.int32),
                pltpu.SemaphoreType.DMA((2, slabs)),
            ],
        ),
        out_shape=jax.ShapeDtypeStruct((devices, half, HEAD_DIM), jnp.bfloat16),
        compiler_params=pltpu.CompilerParams(vmem_limit_bytes=48 * MIB),
        cost_estimate=pl.CostEstimate(
            flops=flops, bytes_accessed=12 * MIB, transcendentals=flops // (4 * HEAD_DIM)
        ),
        name="attend",
    )(where, *parts, own, sib)

    back = lax.all_to_all(attended, axes, split_axis=0, concat_axis=0, tiled=True)
    return pl.pallas_call(
        unpack_kernel,
        grid=(chips_used,),
        in_specs=[pl.BlockSpec((group, half, HEAD_DIM), lambda i: (i, 0, 0))],
        out_specs=pl.BlockSpec((tokens, head_size * HEAD_DIM), lambda i: (0, i)),
        out_shape=jax.ShapeDtypeStruct((tokens, width), jnp.bfloat16),
        name="unpack",
    )(back)


def solution(mesh):
    placed = (
        P(("seq", "head"), None),
        P(("seq", "head"), None),
        P(("seq", "head"), None),
        P("seq", None),
        P("seq"),
    )
    return jax.shard_map(
        local, mesh=mesh, in_specs=placed, out_specs=P(("seq", "head"), None), check_vma=False
    )
```

time: 156 us -> 144 us (0.923)
  blocking collectives: 118 us -> 99.4 us
  waiting for transfers between devices: 0.01 us -> 8.71 us
  Pallas kernels: 36.6 us -> 29.7 us
  starting transfers between devices: 0.31 us -> 6.29 us
    all_gather x1 -> x0, blocking collectives: 19.5 us -> none  [local(): table = lax.all_gather(table, 'seq', axis=0, tiled=True)]
    ppermute x1 -> x7, waiting for transfers between devices: 0.01 us -> 8.71 us  [the longest x3 5.07 us: local(): lax.ppermute(entry, 'seq', [(s, s // GRID_H * GRID_H + (s + d) % GRID_H)...]
    pallas_call x1, Pallas kernels: 27.6 us -> 20.7 us  [local(): pl.pallas_call(functools.partial(attend_kernel, sources=sources, half=hal...]
    ppermute x1 -> x7, starting transfers between devices: 0.31 us -> 6.29 us  [the longest x3 3.65 us: local(): lax.ppermute(in_slab, 'seq', [(s, (s + e * GRID_H) % rows_all) for s in r...]
  transfers between devices with their start and end apart: 1 -> 7, of which waited for: 0 -> 4; matrix products, arithmetic and copies ran while one was open for 0% -> 0% of each run, Pallas kernels for 0% -> 0%
where the time goes in v2:
time: 144 us
  blocking collectives  99.4 us (69%)
  Pallas kernels  29.7 us (21%)
  waiting for transfers between devices  8.71 us (6%)
  starting transfers between devices  6.29 us (4%)
    all_to_all x1, blocking collectives, local(): own = lax.all_to_all(packed, axes, split_axis=0, concat_axis=0, tiled=True)  70.6 us
    all_to_all x1, blocking collectives, local(): lax.all_to_all(attended, axes, split_axis=0, concat_axis=0, tiled=True)  28.7 us
    pallas_call x1, Pallas kernels, local(): pl.pallas_call(functools.partial(attend_kernel, sources=sources, half=hal...  20.7 us
    pallas_call x1, Pallas kernels, local(): pl.pallas_call(pack_kernel, grid=(chips_used,), in_specs=[pl.BlockSpec((t...  5.14 us
    ppermute x3, waiting for transfers between devices, local(): lax.ppermute(entry, 'seq', [(s, s // GRID_H * GRID_H + (s + d) % GRID_H)...  5.07 us
    pallas_call x1, Pallas kernels, local(): pl.pallas_call(unpack_kernel, grid=(chips_used,), in_specs=[pl.BlockSpec(...  3.83 us
    ppermute x3, starting transfers between devices, local(): lax.ppermute(in_slab, 'seq', [(s, (s + e * GRID_H) % rows_all) for s in r...  3.65 us
    ppermute x3, waiting for transfers between devices, local(): lax.ppermute(in_slab, 'seq', [(s, (s + e * GRID_H) % rows_all) for s in r...  3.64 us
  transfers between devices with their start and end apart: 7, of which 4 were waited for; matrix products, arithmetic and copies ran while one was open for 0% of the time, Pallas kernels for 0%

profile of v2, /device:TPU:1, one launch (start us, length us, event | category | flops | bytes accessed | tf_op | source)
XLA Modules:
  0.0 144.3 jit_solution(1258542622839667645)
XLA Ops:
  0.0 5.1 %pack.1 = bf16[128,144,128]{2,1,0:T(8,128)(2,1)} custom-call(bf16[96,5120]{1,0:T(8,128)(2,1)} %q_ref.1, bf16[96,5120]{1,0:T(8,128)(2,1)} %k_ref.1, bf16[96,5120]{1,0:T(8,128)(2,1)} %v_ref.1), custom_call_target="tpu_custom_call" | custom-call | tf_op jit(solution)/shard_map/pack/pallas_call | solution.py:170
  5.1 0.0 copy-start.1
  5.1 0.0 copy-start
  5.1 70.6 %all_to_all.10.refs_5_ = bf16[128,144,128]{2,1,0:T(8,128)(2,1)} all-to-all(bf16[128,144,128]{2,1,0:T(8,128)(2,1)} %pack.1), channel_id=1, replica_groups=mesh['seq'=16,'head'=8] {'seq','head'}, dimensions={0} | all-to-all | bytes 9437184 | tf_op jit(solution)/shard_map/all_to_all | solution.py:178
  75.8 0.3 collective-permute-start.6
  76.1 0.0 copy-done.1
  76.1 0.1 reshape.10
  76.2 0.0 copy-done
  76.2 0.1 pad_add_fusion.1
  76.2 0.2 collective-permute-start.2
  76.4 0.2 collective-permute-start.1
  76.6 1.9 %collective-permute-start = (s32[1,10]{1,0:T(1,128)S(1)}, s32[1,10]{1,0:T(1,128)S(1)}, u32[]{:S(2)}, u32[]{:S(2)}) collective-permute-start(s32[1,10]{1,0:T(1,128)S(1)} %pad_add_fusion.1), channel_id=1, source_target_pairs={{0,8},{8,16},{16,24},{24,0},{32,40},{40,48},{48,56},{56,32},{64,72... | collective-permute-start | bytes 128 | tf_op jit(solution)/shard_map/ppermute | solution.py:161
  78.6 2.0 %collective-permute-done.2 = s32[1,10]{1,0:T(1,128)S(1)} collective-permute-done((s32[1,10]{1,0:T(1,128)S(1)}, s32[1,10]{1,0:T(1,128)S(1)}, u32[]{:S(2)}, u32[]{:S(2)}) %collective-permute-start.2) | collective-permute-done | bytes 72 | tf_op jit(solution)/shard_map/ppermute | solution.py:161
  80.6 0.0 collective-permute-done.1
  80.6 3.1 %collective-permute-done = s32[1,10]{1,0:T(1,128)S(1)} collective-permute-done((s32[1,10]{1,0:T(1,128)S(1)}, s32[1,10]{1,0:T(1,128)S(1)}, u32[]{:S(2)}, u32[]{:S(2)}) %collective-permute-start) | collective-permute-done | bytes 72 | tf_op jit(solution)/shard_map/ppermute | solution.py:161
  83.6 0.1 pad_add_fusion.refs_1_
  83.7 1.2 collective-permute-start.5
  84.9 1.2 collective-permute-start.4
  86.2 1.2 collective-permute-start.3
  87.4 0.3 collective-permute-done.5.refs_4_
  87.7 0.0 collective-permute-done.4.refs_3_
  87.7 3.3 %collective-permute-done.3.refs_2_ = s32[4,10]{1,0:T(4,128)S(1)} collective-permute-done((s32[4,10]{1,0:T(4,128)S(1)}, s32[4,10]{1,0:T(4,128)S(1)}, u32[]{:S(2)}, u32[]{:S(2)}) %collective-permute-start.3) | collective-permute-done | bytes 192 | tf_op jit(solution)/shard_map/ppermute | solution.py:182
  91.0 0.0 collective-permute-done.6.refs_6_
  91.0 20.7 %attend.1 = bf16[128,48,128]{2,1,0:T(8,128)(2,1)S(1)} custom-call(s32[1]{0:T(128)} %bitcast.refs_0_, s32[4,10]{1,0:T(4,128)S(1)} %pad_add_fusion.refs_1_, s32[4,10]{1,0:T(4,128)S(1)} %collective-permute-done.3.refs_2_, s32[4,10]{1,0:T(4,128)S(1)} %collective-permute-done.4.refs_3_, s32[4,10]{1,0:T(4,128)S(1)} %collective-permute-done.5.refs_4_, ...), custom_call_target="tpu_custom_call" | custom-call | flops 4831838208 | bytes 12582912 | tf_op jit(solution)/shard_map/attend/pallas_call | solution.py:189
  111.7 28.7 %all_to_all.11.i_ref = bf16[128,48,128]{2,1,0:T(8,128)(2,1)} all-to-all(bf16[128,48,128]{2,1,0:T(8,128)(2,1)S(1)} %attend.1), channel_id=1, replica_groups=mesh['seq'=16,'head'=8] {'seq','head'}, dimensions={0} | all-to-all | bytes 3145728 | tf_op jit(solution)/shard_map/all_to_all | solution.py:212
  140.5 3.8 %unpack.1 = bf16[96,5120]{1,0:T(8,128)(2,1)} custom-call(bf16[128,48,128]{2,1,0:T(8,128)(2,1)} %all_to_all.11.i_ref), custom_call_target="tpu_custom_call" | custom-call | tf_op jit(solution)/shard_map/unpack/pallas_call | solution.py:213
Async XLA Ops:
  5.1 70.9 %copy-start.1 = (s32[2,4]{1,0:T(2,128)S(1)}, s32[2,4]{1,0:T(2,128)}, u32[]{:S(2)}) copy-start(s32[2,4]{1,0:T(2,128)} %param.8) | copy-start | bytes 100
  5.1 71.0 %copy-start = (s32[2]{0:T(128)S(1)}, s32[2]{0:T(128)}, u32[]{:S(2)}) copy-start(s32[2]{0:T(128)} %param.9) | copy-start | bytes 28
  75.8 15.2 %collective-permute-start.6 = (bf16[128,144,128]{2,1,0:T(8,128)(2,1)}, bf16[128,144,128]{2,1,0:T(8,128)(2,1)}, u32[]{:S(2)}, u32[]{:S(2)}) collective-permute-start(bf16[128,144,128]{2,1,0:T(8,128)(2,1)} %all_to_all.10.refs_5_), channel_id=1, source_target_pairs={{0,8},{8,0},{16,24},{24,16},{32,40},{40,32},{48,56},{56,48},{64,72... | collective-permute-start | bytes 14155784 | tf_op jit(solution)/shard_map/ppermute | solution.py:179
  76.2 4.3 %collective-permute-start.2 = (s32[1,10]{1,0:T(1,128)S(1)}, s32[1,10]{1,0:T(1,128)S(1)}, u32[]{:S(2)}, u32[]{:S(2)}) collective-permute-start(s32[1,10]{1,0:T(1,128)S(1)} %pad_add_fusion.1), channel_id=1, source_target_pairs={{0,24},{8,0},{16,8},{24,16},{32,56},{40,32},{48,40},{56,48},{64,88... | collective-permute-start | bytes 128 | tf_op jit(solution)/shard_map/ppermute | solution.py:161
  76.4 4.1 %collective-permute-start.1 = (s32[1,10]{1,0:T(1,128)S(1)}, s32[1,10]{1,0:T(1,128)S(1)}, u32[]{:S(2)}, u32[]{:S(2)}) collective-permute-start(s32[1,10]{1,0:T(1,128)S(1)} %pad_add_fusion.1), channel_id=1, source_target_pairs={{0,16},{8,24},{16,0},{24,8},{32,48},{40,56},{48,32},{56,40},{64,80... | collective-permute-start | bytes 128 | tf_op jit(solution)/shard_map/ppermute | solution.py:161
  76.6 7.0 %collective-permute-start = (s32[1,10]{1,0:T(1,128)S(1)}, s32[1,10]{1,0:T(1,128)S(1)}, u32[]{:S(2)}, u32[]{:S(2)}) collective-permute-start(s32[1,10]{1,0:T(1,128)S(1)} %pad_add_fusion.1), channel_id=1, source_target_pairs={{0,8},{8,16},{16,24},{24,0},{32,40},{40,48},{48,56},{56,32},{64,72... | collective-permute-start | bytes 128 | tf_op jit(solution)/shard_map/ppermute | solution.py:161
  83.7 3.9 %collective-permute-start.5 = (s32[4,10]{1,0:T(4,128)S(1)}, s32[4,10]{1,0:T(4,128)S(1)}, u32[]{:S(2)}, u32[]{:S(2)}) collective-permute-start(s32[4,10]{1,0:T(4,128)S(1)} %pad_add_fusion.refs_1_), channel_id=1, source_target_pairs={{0,96},{8,104},{16,112},{24,120},{32,0},{40,8},{48,16},{56,24},{64... | collective-permute-start | bytes 488 | tf_op jit(solution)/shard_map/ppermute | solution.py:182
  84.9 2.7 %collective-permute-start.4 = (s32[4,10]{1,0:T(4,128)S(1)}, s32[4,10]{1,0:T(4,128)S(1)}, u32[]{:S(2)}, u32[]{:S(2)}) collective-permute-start(s32[4,10]{1,0:T(4,128)S(1)} %pad_add_fusion.refs_1_), channel_id=1, source_target_pairs={{0,64},{8,72},{16,80},{24,88},{32,96},{40,104},{48,112},{56,120},{... | collective-permute-start | bytes 488 | tf_op jit(solution)/shard_map/ppermute | solution.py:182
  86.2 4.8 %collective-permute-start.3 = (s32[4,10]{1,0:T(4,128)S(1)}, s32[4,10]{1,0:T(4,128)S(1)}, u32[]{:S(2)}, u32[]{:S(2)}) collective-permute-start(s32[4,10]{1,0:T(4,128)S(1)} %pad_add_fusion.refs_1_), channel_id=1, source_target_pairs={{0,32},{8,40},{16,48},{24,56},{32,64},{40,72},{48,80},{56,88},{64,... | collective-permute-start | bytes 488 | tf_op jit(solution)/shard_map/ppermute | solution.py:182

commit v3 on v2

--- a/solution.py
+++ b/solution.py
@@ -25,14 +25,6 @@
             cols = pl.ds(h * HEAD_DIM, HEAD_DIM)
             for part, ref in enumerate((k_ref, v_ref, q_ref)):
                 o_ref[core * heads + h, pl.ds(part * half, half), :] = ref[rows, cols]
-
-
-def unpack_kernel(i_ref, o_ref):
-    half = i_ref.shape[1]
-    heads = i_ref.shape[0] // CORES
-    for core in range(CORES):
-        for h in range(heads):
-            o_ref[pl.ds(core * half, half), pl.ds(h * HEAD_DIM, HEAD_DIM)] = i_ref[core * heads + h]
 
 
 def attend_kernel(*refs, sources, half, slabs):
@@ -173,8 +165,10 @@
         in_specs=[pl.BlockSpec((tokens, head_size * HEAD_DIM), lambda i: (0, i))] * 3,
         out_specs=pl.BlockSpec((group, 3 * half, HEAD_DIM), lambda i: (i, 0, 0)),
         out_shape=jax.ShapeDtypeStruct((devices, 3 * half, HEAD_DIM), jnp.bfloat16),
+        cost_estimate=pl.CostEstimate(flops=0, bytes_accessed=6 * MIB, transcendentals=0),
         name="pack",
     )(queries, keys, values)
+    in_slab, packed = lax.optimization_barrier((in_slab, packed))
     own = lax.all_to_all(packed, axes, split_axis=0, concat_axis=0, tiled=True)
     sib = lax.ppermute(own, "seq", [(s, s ^ 1) for s in range(rows_all)])
     in_slab, own = lax.optimization_barrier((in_slab, own))
@@ -210,14 +204,8 @@
     )(where, *parts, own, sib)
 
     back = lax.all_to_all(attended, axes, split_axis=0, concat_axis=0, tiled=True)
-    return pl.pallas_call(
-        unpack_kernel,
-        grid=(chips_used,),
-        in_specs=[pl.BlockSpec((group, half, HEAD_DIM), lambda i: (i, 0, 0))],
-        out_specs=pl.BlockSpec((tokens, head_size * HEAD_DIM), lambda i: (0, i)),
-        out_shape=jax.ShapeDtypeStruct((tokens, width), jnp.bfloat16),
-        name="unpack",
-    )(back)
+    back = back.reshape(-1, CORES, head_size, half, HEAD_DIM)[:chips_used]
+    return back.transpose(1, 3, 0, 2, 4).reshape(tokens, width)
 
 
 def solution(mesh):

time: 144 us -> 138 us (0.958)
  waiting for transfers between devices: 8.71 us -> 4.44 us
  Pallas kernels: 29.7 us -> 26.3 us
  blocking collectives: 99.4 us -> 96.5 us
  local copies, waits for them, and re-layouts: 0.09 us -> 2.45 us
  starting transfers between devices: 6.29 us -> 7.88 us
    ppermute x3, waiting for transfers between devices: 5.07 us -> 0.01 us  [local(): lax.ppermute(entry, 'seq', [(s, s // GRID_H * GRID_H + (s + d) % GRID_H)...]
    pallas_call x1 -> x0, Pallas kernels: 3.83 us -> none  [local(): pl.pallas_call(unpack_kernel, grid=(chips_used,), in_specs=[pl.BlockSpec(...]
    ppermute x3, starting transfers between devices: 2.33 us -> 4.07 us  [local(): lax.ppermute(entry, 'seq', [(s, s // GRID_H * GRID_H + (s + d) % GRID_H)...]
    all_to_all x1, blocking collectives: 70.6 us -> 68.9 us  [local(): own = lax.all_to_all(packed, axes, split_axis=0, concat_axis=0, tiled=True)]
  transfers between devices with their start and end apart: 7 -> 7, of which waited for: 4 -> 4; matrix products, arithmetic and copies ran while one was open for 0% -> 0% of each run, Pallas kernels for 0% -> 4%
where the time goes in v3:
time: 138 us
  blocking collectives  96.5 us (70%)
  Pallas kernels  26.3 us (19%)
  starting transfers between devices  7.88 us (6%)
  waiting for transfers between devices  4.44 us (3%)
  local copies, waits for them, and re-layouts  2.45 us (2%)
    all_to_all x1, blocking collectives, local(): own = lax.all_to_all(packed, axes, split_axis=0, concat_axis=0, tiled=True)  68.9 us
    all_to_all x1, blocking collectives, local(): lax.all_to_all(attended, axes, split_axis=0, concat_axis=0, tiled=True)  27.6 us
    pallas_call x1, Pallas kernels, local(): pl.pallas_call(functools.partial(attend_kernel, sources=sources, half=hal...  21.1 us
    pallas_call x1, Pallas kernels, local(): pl.pallas_call(pack_kernel, grid=(chips_used,), in_specs=[pl.BlockSpec((t...  5.14 us
    ppermute x3, starting transfers between devices, local(): lax.ppermute(entry, 'seq', [(s, s // GRID_H * GRID_H + (s + d) % GRID_H)...  4.07 us
    ppermute x3, waiting for transfers between devices, local(): lax.ppermute(in_slab, 'seq', [(s, (s + e * GRID_H) % rows_all) for s in r...  3.75 us
    ppermute x3, starting transfers between devices, local(): lax.ppermute(in_slab, 'seq', [(s, (s + e * GRID_H) % rows_all) for s in r...  3.51 us
  transfers between devices with their start and end apart: 7, of which 4 were waited for; matrix products, arithmetic and copies ran while one was open for 0% of the time, Pallas kernels for 4%

profile of v3, /device:TPU:1, one launch (start us, length us, event | category | flops | bytes accessed | tf_op | source)
XLA Modules:
  0.0 138.5 jit_solution(15609075961871592465)
XLA Ops:
  0.0 0.0 copy-start
  0.0 0.8 reshape.15
  0.8 0.7 pad_add_fusion.1
  1.5 1.4 %collective-permute-start.2 = (s32[1,10]{1,0:T(1,128)S(1)}, s32[1,10]{1,0:T(1,128)S(1)}, u32[]{:S(2)}, u32[]{:S(2)}) collective-permute-start(s32[1,10]{1,0:T(1,128)S(1)} %pad_add_fusion.1), channel_id=1, source_target_pairs={{0,24},{8,0},{16,8},{24,16},{32,56},{40,32},{48,40},{56,48},{64,88... | collective-permute-start | bytes 128 | tf_op jit(solution)/shard_map/ppermute | solution.py:153
  2.9 1.3 collective-permute-start.1
  4.2 1.4 collective-permute-start
  5.6 5.1 %pack.1 = bf16[128,144,128]{2,1,0:T(8,128)(2,1)} custom-call(bf16[96,5120]{1,0:T(8,128)(2,1)} %q_ref.1, bf16[96,5120]{1,0:T(8,128)(2,1)} %k_ref.1, bf16[96,5120]{1,0:T(8,128)(2,1)} %v_ref.1), custom_call_target="tpu_custom_call" | custom-call | bytes 6291456 | tf_op jit(solution)/shard_map/pack/pallas_call | solution.py:162
  10.7 0.0 collective-permute-done.2
  10.7 0.0 collective-permute-done.1
  10.7 0.0 collective-permute-done
  10.7 0.0 copy-done
  10.7 0.1 pad_add_fusion.refs_1_
  10.8 68.9 %all_to_all.10.refs_5_ = bf16[128,144,128]{2,1,0:T(8,128)(2,1)} all-to-all(bf16[128,144,128]{2,1,0:T(8,128)(2,1)} %pack.1), channel_id=1, replica_groups=mesh['seq'=16,'head'=8] {'seq','head'}, dimensions={0} | all-to-all | bytes 9437184 | tf_op jit(solution)/shard_map/all_to_all | solution.py:172
  79.8 0.3 collective-permute-start.6
  80.1 1.3 collective-permute-start.5
  81.4 1.1 collective-permute-start.4
  82.5 1.1 collective-permute-start.3
  83.6 0.4 collective-permute-done.5.refs_4_
  84.0 0.1 collective-permute-done.4.refs_3_
  84.1 3.2 %collective-permute-done.3.refs_2_ = s32[4,10]{1,0:T(4,128)S(1)} collective-permute-done((s32[4,10]{1,0:T(4,128)S(1)}, s32[4,10]{1,0:T(4,128)S(1)}, u32[]{:S(2)}, u32[]{:S(2)}) %collective-permute-start.3) | collective-permute-done | bytes 192 | tf_op jit(solution)/shard_map/ppermute | solution.py:176
  87.3 0.7 collective-permute-done.6.refs_6_
  88.0 21.1 %attend.1 = bf16[128,48,128]{2,1,0:T(8,128)(2,1)S(1)} custom-call(s32[1]{0:T(128)} %bitcast.refs_0_, s32[4,10]{1,0:T(4,128)S(1)} %pad_add_fusion.refs_1_, s32[4,10]{1,0:T(4,128)S(1)} %collective-permute-done.3.refs_2_, s32[4,10]{1,0:T(4,128)S(1)} %collective-permute-done.4.refs_3_, s32[4,10]{1,0:T(4,128)S(1)} %collective-permute-done.5.refs_4_, ...), custom_call_target="tpu_custom_call" | custom-call | flops 4831838208 | bytes 12582912 | tf_op jit(solution)/shard_map/attend/pallas_call | solution.py:183
  109.2 27.6 %all_to_all.11 = bf16[128,48,128]{2,1,0:T(8,128)(2,1)S(1)} all-to-all(bf16[128,48,128]{2,1,0:T(8,128)(2,1)S(1)} %attend.1), channel_id=1, replica_groups=mesh['seq'=16,'head'=8] {'seq','head'}, dimensions={0} | all-to-all | bytes 3145728 | tf_op jit(solution)/shard_map/all_to_all | solution.py:206
  136.8 0.1 slice.8
  136.8 0.3 copy.6
  137.1 1.4 reshape.17
Async XLA Ops:
  0.0 10.7 %copy-start = (s32[2]{0:T(128)S(1)}, s32[2]{0:T(128)}, u32[]{:S(2)}) copy-start(s32[2]{0:T(128)} %param.9) | copy-start | bytes 28
  1.5 9.2 %collective-permute-start.2 = (s32[1,10]{1,0:T(1,128)S(1)}, s32[1,10]{1,0:T(1,128)S(1)}, u32[]{:S(2)}, u32[]{:S(2)}) collective-permute-start(s32[1,10]{1,0:T(1,128)S(1)} %pad_add_fusion.1), channel_id=1, source_target_pairs={{0,24},{8,0},{16,8},{24,16},{32,56},{40,32},{48,40},{56,48},{64,88... | collective-permute-start | bytes 128 | tf_op jit(solution)/shard_map/ppermute | solution.py:153
  2.9 7.8 %collective-permute-start.1 = (s32[1,10]{1,0:T(1,128)S(1)}, s32[1,10]{1,0:T(1,128)S(1)}, u32[]{:S(2)}, u32[]{:S(2)}) collective-permute-start(s32[1,10]{1,0:T(1,128)S(1)} %pad_add_fusion.1), channel_id=1, source_target_pairs={{0,16},{8,24},{16,0},{24,8},{32,48},{40,56},{48,32},{56,40},{64,80... | collective-permute-start | bytes 128 | tf_op jit(solution)/shard_map/ppermute | solution.py:153
  4.2 6.5 %collective-permute-start = (s32[1,10]{1,0:T(1,128)S(1)}, s32[1,10]{1,0:T(1,128)S(1)}, u32[]{:S(2)}, u32[]{:S(2)}) collective-permute-start(s32[1,10]{1,0:T(1,128)S(1)} %pad_add_fusion.1), channel_id=1, source_target_pairs={{0,8},{8,16},{16,24},{24,0},{32,40},{40,48},{48,56},{56,32},{64,72... | collective-permute-start | bytes 128 | tf_op jit(solution)/shard_map/ppermute | solution.py:153
  79.8 8.3 %collective-permute-start.6 = (bf16[128,144,128]{2,1,0:T(8,128)(2,1)}, bf16[128,144,128]{2,1,0:T(8,128)(2,1)}, u32[]{:S(2)}, u32[]{:S(2)}) collective-permute-start(bf16[128,144,128]{2,1,0:T(8,128)(2,1)} %all_to_all.10.refs_5_), channel_id=1, source_target_pairs={{0,8},{8,0},{16,24},{24,16},{32,40},{40,32},{48,56},{56,48},{64,72... | collective-permute-start | bytes 14155784 | tf_op jit(solution)/shard_map/ppermute | solution.py:173
  80.1 3.9 %collective-permute-start.5 = (s32[4,10]{1,0:T(4,128)S(1)}, s32[4,10]{1,0:T(4,128)S(1)}, u32[]{:S(2)}, u32[]{:S(2)}) collective-permute-start(s32[4,10]{1,0:T(4,128)S(1)} %pad_add_fusion.refs_1_), channel_id=1, source_target_pairs={{0,96},{8,104},{16,112},{24,120},{32,0},{40,8},{48,16},{56,24},{64... | collective-permute-start | bytes 488 | tf_op jit(solution)/shard_map/ppermute | solution.py:176
  81.4 2.7 %collective-permute-start.4 = (s32[4,10]{1,0:T(4,128)S(1)}, s32[4,10]{1,0:T(4,128)S(1)}, u32[]{:S(2)}, u32[]{:S(2)}) collective-permute-start(s32[4,10]{1,0:T(4,128)S(1)} %pad_add_fusion.refs_1_), channel_id=1, source_target_pairs={{0,64},{8,72},{16,80},{24,88},{32,96},{40,104},{48,112},{56,120},{... | collective-permute-start | bytes 488 | tf_op jit(solution)/shard_map/ppermute | solution.py:176
  82.5 4.8 %collective-permute-start.3 = (s32[4,10]{1,0:T(4,128)S(1)}, s32[4,10]{1,0:T(4,128)S(1)}, u32[]{:S(2)}, u32[]{:S(2)}) collective-permute-start(s32[4,10]{1,0:T(4,128)S(1)} %pad_add_fusion.refs_1_), channel_id=1, source_target_pairs={{0,32},{8,40},{16,48},{24,56},{32,64},{40,72},{48,80},{56,88},{64,... | collective-permute-start | bytes 488 | tf_op jit(solution)/shard_map/ppermute | solution.py:176

commit v4 on v3

v4 whole, which is shorter than its diff:
```python
import functools
import math

import jax
import jax.numpy as jnp
from jax import lax
from jax.experimental import pallas as pl
from jax.experimental.pallas import tpu as pltpu
from jax.sharding import PartitionSpec as P

HEAD_DIM = 128
GRID_H = 4
MAXK = 4
CORES = 2
MIB = 1 << 20


def pack_kernel(q_ref, k_ref, v_ref, o_ref):
    tokens, width = q_ref.shape
    for h in range(width // HEAD_DIM):
        cols = pl.ds(h * HEAD_DIM, HEAD_DIM)
        for part, ref in enumerate((k_ref, v_ref, q_ref)):
            o_ref[h, pl.ds(part * tokens, tokens), :] = ref[:, cols]


def attend_kernel(*refs, sources, slabs):
    where, parts = refs[0], refs[1 : 1 + slabs]
    own_hbm, sib_hbm, o_hbm = refs[1 + slabs : 4 + slabs]
    kv, queries, outs, scores, peaks, table, order, in_sems, out_sems = refs[4 + slabs :]
    tokens = queries.shape[1]
    tile_len = sources * tokens
    tiles = queries.shape[0] // sources
    slab_len = queries.shape[0] // slabs
    slab_tiles = tiles // slabs
    row_tiles = table.shape[0] // (slabs * GRID_H)
    row_len = row_tiles * sources
    core = where[0] % CORES
    factor = math.log2(math.e) / math.sqrt(HEAD_DIM)

    def copies(slab):
        at = pl.ds(slab * slab_len, slab_len)
        keys = pl.ds(0, 2 * tokens)
        return (
            pltpu.make_async_copy(
                own_hbm.at[at, pl.ds(2 * tokens, tokens)], queries.at[at], in_sems.at[0, slab]
            ),
            pltpu.make_async_copy(own_hbm.at[at, keys], kv.at[0, at], in_sems.at[1, slab]),
            pltpu.make_async_copy(sib_hbm.at[at, keys], kv.at[1, at], in_sems.at[2, slab]),
        )

    for slab in range(slabs):
        for copy in copies(slab):
            copy.start()

    my_slab, my_row = where[0] // GRID_H, where[0] % GRID_H
    for e in range(slabs):
        for d in range(GRID_H):
            row = (my_slab + slabs - e) % slabs * GRID_H + (my_row + GRID_H - d) % GRID_H
            for w in range(row_tiles):
                for m in range(MAXK):
                    table[row * row_tiles + w, m] = parts[e][d, w * MAXK + m]
                table[row * row_tiles + w, MAXK] = parts[e][d, row_tiles * MAXK + w]

    def whole(local):
        return (local // row_tiles * CORES + core) * row_tiles + local % row_tiles

    def sort(local, filled):
        full = table[whole(local), MAXK] > MAXK - 1
        n_full, n_less = filled

        @pl.when(full)
        def _():
            order[0, n_full] = local

        @pl.when(jnp.logical_not(full))
        def _():
            order[1, n_less] = local

        step = full.astype(jnp.int32)
        return n_full + step, n_less + 1 - step

    filled = lax.fori_loop(0, tiles, sort, (jnp.int32(0), jnp.int32(0)))

    def loaded(have, need):
        for slab in range(slabs):

            @pl.when(jnp.logical_and(have <= slab, slab < need))
            def _(slab=slab):
                for copy in copies(slab):
                    copy.wait()

        return jnp.maximum(have, need)

    def listed(local, m, part):
        tile = table[whole(local), m]
        row = tile // row_tiles
        side = (row + core) % CORES
        first = row // CORES * row_len + tile % row_tiles * sources
        block = kv[side, pl.ds(first, sources), pl.ds(part * tokens, tokens), :]
        return block.reshape(tile_len, HEAD_DIM)

    def query_of(local):
        return queries[pl.ds(local * sources, sources)].reshape(tile_len, HEAD_DIM)

    def score(local, slot, m, query, peak):
        block = lax.dot_general(
            query, listed(local, m, 0), (((1,), (1,)), ((), ())), preferred_element_type=jnp.float32
        )
        scores[slot, m] = block
        for at in range(0, tile_len, HEAD_DIM):
            part = block[:, at : at + HEAD_DIM]
            peak = part if peak is None else jnp.maximum(peak, part)
        return peak

    def keep_peak(slot, peak):
        peaks[slot] = jnp.broadcast_to(jnp.max(peak, axis=-1, keepdims=True), peak.shape)

    def weigh(local, slot, m, peak, total):
        probs = jnp.exp2((scores[slot, m] - peak) * factor).astype(jnp.bfloat16)
        value = listed(local, m, 1)
        value = jnp.concatenate([value, jnp.ones_like(value)], axis=1)
        return total + jnp.dot(probs, value, preferred_element_type=jnp.float32)

    def sent(local):
        at = pl.ds(local * sources, sources)
        return pltpu.make_async_copy(outs.at[at], o_hbm.at[at], out_sems.at[local])

    def pair(this, this_slot, then, then_slot, count, fresh):
        total = jnp.zeros((tile_len, 2 * HEAD_DIM), jnp.float32)
        peak = jnp.concatenate([peaks[this_slot]] * (tile_len // HEAD_DIM), axis=1)
        query, then_peak = query_of(then), None
        for m in range(count):
            then_peak = score(then, then_slot, m, query, then_peak)
            total = weigh(this, this_slot, m, peak, total)
        keep_peak(then_slot, then_peak)
        out = (total[:, :HEAD_DIM] / total[:, HEAD_DIM:]).astype(outs.dtype)
        place = this if fresh is None else jnp.where(fresh, this, tiles)
        outs[pl.ds(place * sources, sources)] = out.reshape(sources, tokens, HEAD_DIM)
        if fresh is None:
            sent(this).start()
        else:
            pl.when(fresh)(lambda: sent(this).start())

    def need(local):
        return jnp.minimum(local // slab_tiles + 2, slabs)

    have = jnp.int32(0)
    for kind, count in enumerate((MAXK, MAXK - 1)):
        number = filled[kind]

        def pick(i, kind=kind, number=number):
            return order[kind, jnp.minimum(i, number - 1)]

        def first(have, count=count, pick=pick):
            local = pick(0)
            have = loaded(have, need(local))
            query, peak = query_of(local), None
            for m in range(count):
                peak = score(local, 0, m, query, peak)
            keep_peak(0, peak)
            return have

        have = lax.cond(number > 0, first, lambda have: have, have)

        def step(i, have, count=count, pick=pick, number=number):
            a, b, c = pick(2 * i), pick(2 * i + 1), pick(2 * i + 2)
            have = loaded(have, need(c))
            pair(a, 0, b, 1, count, None)
            pair(b, 1, c, 0, count, 2 * i + 1 < number)
            return have

        have = lax.fori_loop(0, (number + 1) // 2, step, have)
    loaded(have, slabs)
    for local in range(tiles):
        sent(local).wait()


def local(queries, keys, values, pairs, pair_count):
    axes = ("seq", "head")
    rows_all = lax.axis_size("seq")
    head_size = lax.axis_size("head")
    devices = rows_all * head_size
    tokens, width = queries.shape
    heads = width // HEAD_DIM
    row_tiles = pairs.shape[0]
    tiles = row_tiles * rows_all
    sources = devices // tiles
    slabs = rows_all // GRID_H
    chips = devices // CORES
    same_core = [
        [s * head_size + h for s in range(core, rows_all, CORES) for h in range(head_size)]
        for core in range(CORES)
    ]

    entry = jnp.concatenate([pairs.reshape(1, -1), pair_count.reshape(1, -1)], axis=1)
    in_slab = [entry] + [
        lax.ppermute(
            entry,
            "seq",
            [(s, s // GRID_H * GRID_H + (s + d) % GRID_H) for s in range(rows_all)],
        )
        for d in range(1, GRID_H)
    ]
    in_slab = jnp.concatenate(in_slab, axis=0)

    packed = pl.pallas_call(
        pack_kernel,
        grid=(heads // head_size,),
        in_specs=[pl.BlockSpec((tokens, head_size * HEAD_DIM), lambda i: (0, i))] * 3,
        out_specs=pl.BlockSpec((head_size, 3 * tokens, HEAD_DIM), lambda i: (i, 0, 0)),
        out_shape=jax.ShapeDtypeStruct((chips, 3 * tokens, HEAD_DIM), jnp.bfloat16),
        cost_estimate=pl.CostEstimate(flops=0, bytes_accessed=6 * MIB, transcendentals=0),
        name="pack",
    )(queries, keys, values)
    in_slab, packed = lax.optimization_barrier((in_slab, packed))
    own = lax.all_to_all(
        packed, axes, split_axis=0, concat_axis=0, tiled=True, axis_index_groups=same_core
    )
    sib = lax.ppermute(own, "seq", [(s, s ^ 1) for s in range(rows_all)])
    in_slab, own = lax.optimization_barrier((in_slab, own))
    parts = [in_slab] + [
        lax.ppermute(in_slab, "seq", [(s, (s + e * GRID_H) % rows_all) for s in range(rows_all)])
        for e in range(1, slabs)
    ]
    where = lax.axis_index("seq").astype(jnp.int32).reshape(1)

    tile_len = sources * tokens
    flops = 4 * (tiles // CORES) * tile_len * MAXK * tile_len * HEAD_DIM
    anywhere = pl.BlockSpec(memory_space=pl.ANY)
    attended = pl.pallas_call(
        functools.partial(attend_kernel, sources=sources, slabs=slabs),
        grid_spec=pltpu.PrefetchScalarGridSpec(
            num_scalar_prefetch=1 + slabs,
            grid=(1,),
            in_specs=[anywhere, anywhere],
            out_specs=anywhere,
            scratch_shapes=[
                pltpu.VMEM((CORES, chips, 2 * tokens, HEAD_DIM), jnp.bfloat16),
                pltpu.VMEM((chips, tokens, HEAD_DIM), jnp.bfloat16),
                pltpu.VMEM((chips + sources, tokens, HEAD_DIM), jnp.bfloat16),
                pltpu.VMEM((2, MAXK, tile_len, tile_len), jnp.float32),
                pltpu.VMEM((2, tile_len, HEAD_DIM), jnp.float32),
                pltpu.SMEM((tiles, MAXK + 1), jnp.int32),
                pltpu.SMEM((2, tiles // CORES), jnp.int32),
                pltpu.SemaphoreType.DMA((3, slabs)),
                pltpu.SemaphoreType.DMA((tiles // CORES,)),
            ],
        ),
        out_shape=jax.ShapeDtypeStruct((chips, tokens, HEAD_DIM), jnp.bfloat16),
        compiler_params=pltpu.CompilerParams(vmem_limit_bytes=48 * MIB),
        cost_estimate=pl.CostEstimate(
            flops=flops, bytes_accessed=12 * MIB, transcendentals=flops // (4 * HEAD_DIM)
        ),
        name="attend",
    )(where, *parts, own, sib)

    back = lax.all_to_all(
        attended, axes, split_axis=0, concat_axis=0, tiled=True, axis_index_groups=same_core
    )
    return back[:heads].transpose(1, 0, 2).reshape(tokens, width)


def solution(mesh):
    placed = (
        P(("seq", "head"), None),
        P(("seq", "head"), None),
        P(("seq", "head"), None),
        P("seq", None),
        P("seq"),
    )
    return jax.shard_map(
        local, mesh=mesh, in_specs=placed, out_specs=P(("seq", "head"), None), check_vma=False
    )
```

time: 138 us -> 149 us (1.080)
  Pallas kernels: 26.3 us -> 32.9 us
  blocking collectives: 96.5 us -> 101 us
    pallas_call x2, Pallas kernels: 26.3 us -> 32.9 us  [the longest x1 27.7 us: local(): pl.pallas_call(functools.partial(attend_kernel, sources=sources, slabs=sl...]
    all_to_all x2, blocking collectives: 96.5 us -> 101 us  [the longest x1 69.3 us: local(): lax.all_to_all(packed, axes, split_axis=0, concat_axis=0, tiled=True, axi...]
  transfers between devices with their start and end apart: 7 -> 7, of which waited for: 4 -> 4; matrix products, arithmetic and copies ran while one was open for 0% -> 0% of each run, Pallas kernels for 4% -> 3%
where the time goes in v4:
time: 149 us
  blocking collectives  101 us (68%)
  Pallas kernels  32.9 us (22%)
  starting transfers between devices  7.93 us (5%)
  waiting for transfers between devices  4.55 us (3%)
  local copies, waits for them, and re-layouts  1.79 us (1%)
    all_to_all x1, blocking collectives, local(): lax.all_to_all(packed, axes, split_axis=0, concat_axis=0, tiled=True, axi...  69.3 us
    all_to_all x1, blocking collectives, local(): lax.all_to_all(attended, axes, split_axis=0, concat_axis=0, tiled=True, a...  31.9 us
    pallas_call x1, Pallas kernels, local(): pl.pallas_call(functools.partial(attend_kernel, sources=sources, slabs=sl...  27.7 us
    pallas_call x1, Pallas kernels, local(): pl.pallas_call(pack_kernel, grid=(heads // head_size,), in_specs=[pl.Bloc...  5.14 us
    ppermute x3, waiting for transfers between devices, local(): lax.ppermute(in_slab, 'seq', [(s, (s + e * GRID_H) % rows_all) for s in r...  4.23 us
    ppermute x3, starting transfers between devices, local(): lax.ppermute(entry, 'seq', [(s, s // GRID_H * GRID_H + (s + d) % GRID_H)...  4.07 us
    ppermute x3, starting transfers between devices, local(): lax.ppermute(in_slab, 'seq', [(s, (s + e * GRID_H) % rows_all) for s in r...  3.33 us
  transfers between devices with their start and end apart: 7, of which 4 were waited for; matrix products, arithmetic and copies ran while one was open for 0% of the time, Pallas kernels for 3%

profile of v4, /device:TPU:1, one launch (start us, length us, event | category | flops | bytes accessed | tf_op | source)
XLA Modules:
  0.0 149.2 jit_solution(8302768898343701609)
XLA Ops:
  0.0 0.8 reshape.13
  0.8 0.7 pad_add_fusion.1
  1.5 0.0 copy-start
  1.5 1.4 collective-permute-start.2
  2.9 1.3 collective-permute-start.1
  4.2 1.3 collective-permute-start
  5.6 5.1 %pack.1 = bf16[64,288,128]{2,1,0:T(8,128)(2,1)} custom-call(bf16[96,5120]{1,0:T(8,128)(2,1)} %q_ref.1, bf16[96,5120]{1,0:T(8,128)(2,1)} %k_ref.1, bf16[96,5120]{1,0:T(8,128)(2,1)} %v_ref.1), custom_call_target="tpu_custom_call" | custom-call | bytes 6291456 | tf_op jit(solution)/shard_map/pack/pallas_call | solution.py:206
  10.7 0.0 collective-permute-done.2
  10.7 0.0 collective-permute-done.1
  10.7 0.0 collective-permute-done
  10.7 0.0 copy-done
  10.7 0.1 pad_add_fusion.refs_1_
  10.8 69.3 %all_to_all.10.refs_5_ = bf16[64,288,128]{2,1,0:T(8,128)(2,1)} all-to-all(bf16[64,288,128]{2,1,0:T(8,128)(2,1)} %pack.1), channel_id=1, replica_groups={{0,1,2,3,4,5,6,7,16,17,18,19,20,21,22,23,32,33,34,35,36,37,38,39,48,49,..., dimensions={0} | all-to-all | bytes 9437184 | tf_op jit(solution)/shard_map/all_to_all | solution.py:216
  80.1 0.5 collective-permute-start.6
  80.6 2.6 %collective-permute-start.5 = (s32[4,10]{1,0:T(4,128)S(1)}, s32[4,10]{1,0:T(4,128)S(1)}, u32[]{:S(2)}, u32[]{:S(2)}) collective-permute-start(s32[4,10]{1,0:T(4,128)S(1)} %pad_add_fusion.refs_1_), channel_id=1, source_target_pairs={{0,96},{8,104},{16,112},{24,120},{32,0},{40,8},{48,16},{56,24},{64... | collective-permute-start | bytes 488 | tf_op jit(solution)/shard_map/ppermute | solution.py:222
  83.3 0.1 collective-permute-start.4
  83.4 0.6 collective-permute-start.3
  84.0 0.6 collective-permute-done.5.refs_4_
  84.6 1.1 collective-permute-done.4.refs_3_
  85.7 2.5 %collective-permute-done.3.refs_2_ = s32[4,10]{1,0:T(4,128)S(1)} collective-permute-done((s32[4,10]{1,0:T(4,128)S(1)}, s32[4,10]{1,0:T(4,128)S(1)}, u32[]{:S(2)}, u32[]{:S(2)}) %collective-permute-start.3) | collective-permute-done | bytes 192 | tf_op jit(solution)/shard_map/ppermute | solution.py:222
  88.2 0.3 collective-permute-done.6.refs_6_
  88.5 27.7 %attend.1 = bf16[64,96,128]{2,1,0:T(8,128)(2,1)S(1)} custom-call(s32[1]{0:T(128)} %bitcast.refs_0_, s32[4,10]{1,0:T(4,128)S(1)} %pad_add_fusion.refs_1_, s32[4,10]{1,0:T(4,128)S(1)} %collective-permute-done.3.refs_2_, s32[4,10]{1,0:T(4,128)S(1)} %collective-permute-done.4.refs_3_, s32[4,10]{1,0:T(4,128)S(1)} %collective-permute-done.5.refs_4_, ...), custom_call_target="tpu_custom_call" | custom-call | flops 4831838208 | bytes 12582912 | tf_op jit(solution)/shard_map/attend/pallas_call | solution.py:230
  116.3 31.9 %all_to_all.11 = bf16[64,96,128]{2,1,0:T(8,128)(2,1)S(1)} all-to-all(bf16[64,96,128]{2,1,0:T(8,128)(2,1)S(1)} %attend.1), channel_id=1, replica_groups={{0,1,2,3,4,5,6,7,16,17,18,19,20,21,22,23,32,33,34,35,36,37,38,39,48,49,..., dimensions={0} | all-to-all | bytes 3145728 | tf_op jit(solution)/shard_map/all_to_all | solution.py:257
  148.2 1.0 copy_bitcast_fusion
Async XLA Ops:
  1.5 9.2 %copy-start = (s32[2]{0:T(128)S(1)}, s32[2]{0:T(128)}, u32[]{:S(2)}) copy-start(s32[2]{0:T(128)} %param.9) | copy-start | bytes 28
  1.5 9.2 %collective-permute-start.2 = (s32[1,10]{1,0:T(1,128)S(1)}, s32[1,10]{1,0:T(1,128)S(1)}, u32[]{:S(2)}, u32[]{:S(2)}) collective-permute-start(s32[1,10]{1,0:T(1,128)S(1)} %pad_add_fusion.1), channel_id=1, source_target_pairs={{0,24},{8,0},{16,8},{24,16},{32,56},{40,32},{48,40},{56,48},{64,88... | collective-permute-start | bytes 128 | tf_op jit(solution)/shard_map/ppermute | solution.py:197
  2.9 7.8 %collective-permute-start.1 = (s32[1,10]{1,0:T(1,128)S(1)}, s32[1,10]{1,0:T(1,128)S(1)}, u32[]{:S(2)}, u32[]{:S(2)}) collective-permute-start(s32[1,10]{1,0:T(1,128)S(1)} %pad_add_fusion.1), channel_id=1, source_target_pairs={{0,16},{8,24},{16,0},{24,8},{32,48},{40,56},{48,32},{56,40},{64,80... | collective-permute-start | bytes 128 | tf_op jit(solution)/shard_map/ppermute | solution.py:197
  4.2 6.5 %collective-permute-start = (s32[1,10]{1,0:T(1,128)S(1)}, s32[1,10]{1,0:T(1,128)S(1)}, u32[]{:S(2)}, u32[]{:S(2)}) collective-permute-start(s32[1,10]{1,0:T(1,128)S(1)} %pad_add_fusion.1), channel_id=1, source_target_pairs={{0,8},{8,16},{16,24},{24,0},{32,40},{40,48},{48,56},{56,32},{64,72... | collective-permute-start | bytes 128 | tf_op jit(solution)/shard_map/ppermute | solution.py:197
  80.1 8.4 %collective-permute-start.6 = (bf16[64,288,128]{2,1,0:T(8,128)(2,1)}, bf16[64,288,128]{2,1,0:T(8,128)(2,1)}, u32[]{:S(2)}, u32[]{:S(2)}) collective-permute-start(bf16[64,288,128]{2,1,0:T(8,128)(2,1)} %all_to_all.10.refs_5_), channel_id=1, source_target_pairs={{0,8},{8,0},{16,24},{24,16},{32,40},{40,32},{48,56},{56,48},{64,72... | collective-permute-start | bytes 14155784 | tf_op jit(solution)/shard_map/ppermute | solution.py:219
  80.6 3.9 %collective-permute-start.5 = (s32[4,10]{1,0:T(4,128)S(1)}, s32[4,10]{1,0:T(4,128)S(1)}, u32[]{:S(2)}, u32[]{:S(2)}) collective-permute-start(s32[4,10]{1,0:T(4,128)S(1)} %pad_add_fusion.refs_1_), channel_id=1, source_target_pairs={{0,96},{8,104},{16,112},{24,120},{32,0},{40,8},{48,16},{56,24},{64... | collective-permute-start | bytes 488 | tf_op jit(solution)/shard_map/ppermute | solution.py:222
  83.3 2.4 %collective-permute-start.4 = (s32[4,10]{1,0:T(4,128)S(1)}, s32[4,10]{1,0:T(4,128)S(1)}, u32[]{:S(2)}, u32[]{:S(2)}) collective-permute-start(s32[4,10]{1,0:T(4,128)S(1)} %pad_add_fusion.refs_1_), channel_id=1, source_target_pairs={{0,64},{8,72},{16,80},{24,88},{32,96},{40,104},{48,112},{56,120},{... | collective-permute-start | bytes 488 | tf_op jit(solution)/shard_map/ppermute | solution.py:222
  83.4 4.8 %collective-permute-start.3 = (s32[4,10]{1,0:T(4,128)S(1)}, s32[4,10]{1,0:T(4,128)S(1)}, u32[]{:S(2)}, u32[]{:S(2)}) collective-permute-start(s32[4,10]{1,0:T(4,128)S(1)} %pad_add_fusion.refs_1_), channel_id=1, source_target_pairs={{0,32},{8,40},{16,48},{24,56},{32,64},{40,72},{48,80},{56,88},{64,... | collective-permute-start | bytes 488 | tf_op jit(solution)/shard_map/ppermute | solution.py:222

commit v5 on v4

v5 whole, which is shorter than its diff:
```python
import functools
import math

import jax
import jax.numpy as jnp
from jax import lax
from jax.experimental import pallas as pl
from jax.experimental.pallas import tpu as pltpu
from jax.sharding import PartitionSpec as P

HEAD_DIM = 128
GRID_H = 4
MAXK = 4
CORES = 2
TABLE_ROWS = 16
PACK_STEPS = 2
MIB = 1 << 20


def pack_kernel(q_ref, k_ref, v_ref, pairs_ref, count_ref, o_ref, table):
    tokens, width = q_ref.shape
    row_tiles = pairs_ref.shape[0]
    table[...] = jnp.zeros_like(table)
    table[pl.ds(0, row_tiles), pl.ds(0, MAXK)] = pairs_ref[...].astype(jnp.float32)
    table[pl.ds(row_tiles, 1), pl.ds(0, row_tiles)] = count_ref[...].astype(jnp.float32)
    for h in range(width // HEAD_DIM):
        cols = pl.ds(h * HEAD_DIM, HEAD_DIM)
        for part, ref in enumerate((k_ref, v_ref, q_ref)):
            o_ref[h, pl.ds(part * tokens, tokens), :] = ref[:, cols]
        o_ref[h, pl.ds(3 * tokens, TABLE_ROWS), :] = table[...].astype(jnp.bfloat16)


def attend_kernel(own_hbm, sib_hbm, o_hbm, *scratch, row_len, row_tiles, slabs):
    kv, queries, outs, scores, peaks, totals, rows_in, rows_int, table, place, order = scratch[:11]
    in_sems, out_sems, row_sems, table_sem = scratch[11:]
    chips, tokens, _ = queries.shape
    sources = row_len // row_tiles
    tile_len = sources * tokens
    tiles = chips // sources
    slab_len = chips // slabs
    slab_tiles = tiles // slabs
    core = lax.axis_index("seq") % CORES
    factor = math.log2(math.e) / math.sqrt(HEAD_DIM)

    def copies(slab):
        at = pl.ds(slab * slab_len, slab_len)
        beside = pl.ds(chips + slab * slab_len, slab_len)
        return (
            pltpu.make_async_copy(
                own_hbm.at[at, pl.ds(2 * tokens, tokens)], queries.at[at], in_sems.at[0, slab]
            ),
            pltpu.make_async_copy(
                own_hbm.at[at, pl.ds(0, 2 * tokens)], kv.at[at], in_sems.at[1, slab]
            ),
            pltpu.make_async_copy(sib_hbm.at[at], kv.at[beside], in_sems.at[2, slab]),
        )

    fetches = [
        pltpu.make_async_copy(
            own_hbm.at[row * row_len, pl.ds(3 * tokens, TABLE_ROWS)],
            rows_in.at[row],
            row_sems.at[row],
        )
        for row in range(chips // row_len)
    ]
    for fetch in fetches:
        fetch.start()
    for slab in range(2):
        for copy in copies(slab):
            copy.start()
    for fetch in fetches:
        fetch.wait()
    rows_int[...] = rows_in[...].astype(jnp.float32)[:, : rows_int.shape[1]].astype(jnp.int32)
    spread = pltpu.make_async_copy(rows_int, table, table_sem.at[0])
    spread.start()
    spread.wait()

    def sort(local, filled):
        at, w = local // row_tiles, local % row_tiles
        for m in range(MAXK):
            tile = jnp.clip(table[at, w, m], 0, CORES * tiles - 1)
            row = tile // row_tiles
            side = (row + core) % CORES
            place[local, m] = side * chips + row // CORES * row_len + tile % row_tiles * sources
        full = table[at, row_tiles, w] > MAXK - 1
        n_full, n_less = filled

        @pl.when(full)
        def _():
            order[0, n_full] = local

        @pl.when(jnp.logical_not(full))
        def _():
            order[1, n_less] = local

        step = full.astype(jnp.int32)
        return n_full + step, n_less + 1 - step

    filled = lax.fori_loop(0, tiles, sort, (jnp.int32(0), jnp.int32(0)))

    def loaded(have, need):
        for slab in range(slabs):

            @pl.when(jnp.logical_and(have <= slab, slab < need))
            def _(slab=slab):
                for copy in copies(slab):
                    copy.wait()

        return jnp.maximum(have, need)

    def listed(local, m, part):
        block = kv[pl.ds(place[local, m], sources), pl.ds(part * tokens, tokens), :]
        return block.reshape(tile_len, HEAD_DIM)

    def query_of(local):
        return queries[pl.ds(local * sources, sources)].reshape(tile_len, HEAD_DIM)

    def score(local, m, query, peak):
        block = lax.dot_general(
            query, listed(local, m, 0), (((1,), (1,)), ((), ())), preferred_element_type=jnp.float32
        )
        scores[m] = block
        for at in range(0, tile_len, HEAD_DIM):
            part = block[:, at : at + HEAD_DIM]
            peak = part if peak is None else jnp.maximum(peak, part)
        return peak

    def weigh(local, m, peak, total):
        probs = jnp.exp2((scores[m] - peak) * factor).astype(jnp.bfloat16)
        value = listed(local, m, 1)
        value = jnp.concatenate([value, jnp.ones_like(value)], axis=1)
        return total + jnp.dot(probs, value, preferred_element_type=jnp.float32)

    def sent(local):
        at = pl.ds(local * sources, sources)
        return pltpu.make_async_copy(outs.at[at], o_hbm.at[at], out_sems.at[local])

    def finish(local):
        out = totals[:, :HEAD_DIM] / totals[:, HEAD_DIM:]
        outs[pl.ds(local * sources, sources)] = out.astype(outs.dtype).reshape(
            sources, tokens, HEAD_DIM
        )

    def pair(before, this, then, count):
        query = query_of(then)
        finish(before)
        peak = jnp.max(peaks[...], axis=-1, keepdims=True)
        peak = jnp.broadcast_to(peak, (tile_len, tile_len))
        total = jnp.zeros((tile_len, 2 * HEAD_DIM), jnp.float32)
        then_peak = None
        for m in range(count):
            total = weigh(this, m, peak, total)
            then_peak = score(then, m, query, then_peak)
        peaks[...] = then_peak
        totals[...] = total

    def need(local):
        return jnp.minimum(local // slab_tiles + 2, slabs)

    have = loaded(jnp.int32(0), 2)
    for slab in range(2, slabs):
        for copy in copies(slab):
            copy.start()
    for kind, count in enumerate((MAXK, MAXK - 1)):
        number = filled[kind]

        def pick(i, kind=kind, number=number):
            return order[kind, jnp.minimum(i, number - 1)]

        def first(have, count=count, pick=pick):
            local = pick(0)
            have = loaded(have, need(local))
            query, peak = query_of(local), None
            for m in range(count):
                peak = score(local, m, query, peak)
            peaks[...] = peak
            return have

        have = lax.cond(number > 0, first, lambda have: have, have)

        def step(i, have, count=count, pick=pick):
            before, this, then = pick(jnp.maximum(i - 1, 0)), pick(i), pick(i + 1)
            have = loaded(have, need(then))
            pair(before, this, then, count)
            pl.when(i > 0)(lambda: sent(before).start())
            return have

        have = lax.fori_loop(0, number, step, have)

        @pl.when(number > 0)
        def _(pick=pick, number=number):
            finish(pick(number - 1))
            sent(pick(number - 1)).start()

    loaded(have, slabs)
    for local in range(tiles):
        sent(local).wait()


def attend_call(own, sib, *, row_len, row_tiles, slabs):
    chips, tokens = own.shape[0], sib.shape[1] // 2
    sources = row_len // row_tiles
    tiles = chips // sources
    tile_len = sources * tokens
    flops = 4 * tiles * tile_len * MAXK * tile_len * HEAD_DIM
    anywhere = pl.BlockSpec(memory_space=pl.ANY)
    return pl.pallas_call(
        functools.partial(attend_kernel, row_len=row_len, row_tiles=row_tiles, slabs=slabs),
        in_specs=[anywhere, anywhere],
        out_specs=anywhere,
        scratch_shapes=[
            pltpu.VMEM((CORES * chips, 2 * tokens, HEAD_DIM), jnp.bfloat16),
            pltpu.VMEM((chips, tokens, HEAD_DIM), jnp.bfloat16),
            pltpu.VMEM((chips, tokens, HEAD_DIM), jnp.bfloat16),
            pltpu.VMEM((MAXK, tile_len, tile_len), jnp.float32),
            pltpu.VMEM((tile_len, HEAD_DIM), jnp.float32),
            pltpu.VMEM((tile_len, 2 * HEAD_DIM), jnp.float32),
            pltpu.VMEM((chips // row_len, TABLE_ROWS, HEAD_DIM), jnp.bfloat16),
            pltpu.VMEM((chips // row_len, 8, HEAD_DIM), jnp.int32),
            pltpu.SMEM((chips // row_len, 8, HEAD_DIM), jnp.int32),
            pltpu.SMEM((tiles, MAXK), jnp.int32),
            pltpu.SMEM((2, tiles), jnp.int32),
            pltpu.SemaphoreType.DMA((3, slabs)),
            pltpu.SemaphoreType.DMA((tiles,)),
            pltpu.SemaphoreType.DMA((chips // row_len,)),
            pltpu.SemaphoreType.DMA((1,)),
        ],
        out_shape=jax.ShapeDtypeStruct((chips, tokens, HEAD_DIM), jnp.bfloat16),
        compiler_params=pltpu.CompilerParams(vmem_limit_bytes=48 * MIB),
        cost_estimate=pl.CostEstimate(
            flops=flops, bytes_accessed=12 * MIB, transcendentals=flops // (4 * HEAD_DIM)
        ),
        name="attend",
    )(own, sib)


def local(queries, keys, values, pairs, pair_count):
    axes = ("seq", "head")
    rows_all = lax.axis_size("seq")
    head_size = lax.axis_size("head")
    tokens, width = queries.shape
    heads = width // HEAD_DIM
    row_tiles = pairs.shape[0]
    chips = rows_all * head_size // CORES
    slot = 3 * tokens + TABLE_ROWS
    same_core = [
        [s * head_size + h for s in range(core, rows_all, CORES) for h in range(head_size)]
        for core in range(CORES)
    ]

    some = heads // PACK_STEPS
    packed = pl.pallas_call(
        pack_kernel,
        grid=(PACK_STEPS,),
        in_specs=[pl.BlockSpec((tokens, some * HEAD_DIM), lambda i: (0, i))] * 3
        + [
            pl.BlockSpec((row_tiles, MAXK), lambda i: (0, 0)),
            pl.BlockSpec((1, row_tiles), lambda i: (0, 0)),
        ],
        out_specs=pl.BlockSpec((some, slot, HEAD_DIM), lambda i: (i, 0, 0)),
        out_shape=jax.ShapeDtypeStruct((chips, slot, HEAD_DIM), jnp.bfloat16),
        scratch_shapes=[pltpu.VMEM((TABLE_ROWS, HEAD_DIM), jnp.float32)],
        compiler_params=pltpu.CompilerParams(vmem_limit_bytes=32 * MIB),
        name="pack",
    )(queries, keys, values, pairs, pair_count.reshape(1, row_tiles))
    own = lax.all_to_all(
        packed, axes, split_axis=0, concat_axis=0, tiled=True, axis_index_groups=same_core
    )
    swap = [(s, s ^ 1) for s in range(rows_all)]
    sib = lax.ppermute(own[:, : 2 * tokens], "seq", swap)
    attended = attend_call(
        own, sib, row_len=head_size, row_tiles=row_tiles, slabs=rows_all // GRID_H
    )
    back = lax.all_to_all(
        attended, axes, split_axis=0, concat_axis=0, tiled=True, axis_index_groups=same_core
    )
    return back[:heads].transpose(1, 0, 2).reshape(tokens, width)


def solution(mesh):
    placed = (
        P(("seq", "head"), None),
        P(("seq", "head"), None),
        P(("seq", "head"), None),
        P("seq", None),
        P("seq"),
    )
    return jax.shard_map(
        local, mesh=mesh, in_specs=placed, out_specs=P(("seq", "head"), None), check_vma=False
    )
```

time: 149 us -> 139 us (0.933)
  Pallas kernels: 32.9 us -> 23.4 us
  local copies, waits for them, and re-layouts: 1.79 us -> 8.18 us
  starting transfers between devices: 7.93 us -> 2.51 us
  blocking collectives: 101 us -> 99.5 us
    pallas_call x2, Pallas kernels: 32.9 us -> 23.4 us  [the longest x1 21.5 us: attend_call(): pl.pallas_call(functools.partial(attend_kernel, row_len=row_len, row_tile...]
    unnamed x2 -> x12, local copies, waits for them, and re-layouts: 0.01 us -> 6.75 us
    ppermute x7 -> x1, starting transfers between devices: 7.93 us -> 2.51 us  [local(): sib = lax.ppermute(own[:, :2 * tokens], 'seq', swap)]
    all_to_all x1, blocking collectives: 31.9 us -> 28.5 us  [local(): lax.all_to_all(attended, axes, split_axis=0, concat_axis=0, tiled=True, a...]
    all_to_all x1, blocking collectives: 69.3 us -> 71.1 us  [local(): lax.all_to_all(packed, axes, split_axis=0, concat_axis=0, tiled=True, axi...]
    ppermute x7 -> x1, waiting for transfers between devices: 4.55 us -> 5.29 us  [local(): sib = lax.ppermute(own[:, :2 * tokens], 'seq', swap)]
  transfers between devices with their start and end apart: 7 -> 1, of which waited for: 4 -> 1; matrix products, arithmetic and copies ran while one was open for 0% -> 0% of each run, Pallas kernels for 3% -> 0%
where the time goes in v5:
time: 139 us
  blocking collectives  99.5 us (72%)
  Pallas kernels  23.4 us (17%)
  local copies, waits for them, and re-layouts  8.18 us (6%)
  waiting for transfers between devices  5.29 us (4%)
  starting transfers between devices  2.51 us (2%)
    all_to_all x1, blocking collectives, local(): lax.all_to_all(packed, axes, split_axis=0, concat_axis=0, tiled=True, axi...  71.1 us
    all_to_all x1, blocking collectives, local(): lax.all_to_all(attended, axes, split_axis=0, concat_axis=0, tiled=True, a...  28.5 us
    pallas_call x1, Pallas kernels, attend_call(): pl.pallas_call(functools.partial(attend_kernel, row_len=row_len, row_tile...  21.5 us
    unnamed x12, local copies, waits for them, and re-layouts  6.75 us
    ppermute x1, waiting for transfers between devices, local(): sib = lax.ppermute(own[:, :2 * tokens], 'seq', swap)  5.29 us
  transfers between devices with their start and end apart: 1, of which 1 were waited for; matrix products, arithmetic and copies ran while one was open for 0% of the time, Pallas kernels for 0%

profile of v5, /device:TPU:1, one launch (start us, length us, event | category | flops | bytes accessed | tf_op | source)
XLA Modules:
  0.0 139.0 jit_solution(15579594755535832681)
XLA Ops:
  0.0 0.0 copy-start
  0.0 1.2 copy-done
  1.2 0.0 copy-start.1
  1.2 1.2 copy-done.1
  2.4 0.0 copy-start.2
  2.4 1.2 copy-done.2
  3.6 0.0 copy-start.3
  3.6 0.7 copy-done.3
  4.3 0.0 copy-start.4
  4.3 0.7 copy-done.4
  4.9 2.0 %pack.1 = bf16[64,304,128]{2,1,0:T(8,128)(2,1)S(1)} custom-call(bf16[96,5120]{1,0:T(8,128)(2,1)S(1)} %copy-done, bf16[96,5120]{1,0:T(8,128)(2,1)S(1)} %copy-done.1, bf16[96,5120]{1,0:T(8,128)(2,1)S(1)} %copy-done.2, s32[2,4]{1,0:T(2,128)S(1)} %copy-done.3, s32[1,2]{1,0:T(1,128)S(1)} %bitcast.7), custom_call_target="tpu_custom_call" | custom-call | tf_op jit(solution)/shard_map/pack/pallas_call | solution.py:252
  6.9 71.1 %all_to_all.10.own_hbm = bf16[64,304,128]{2,1,0:T(8,128)(2,1)S(1)} all-to-all(bf16[64,304,128]{2,1,0:T(8,128)(2,1)S(1)} %pack.1), channel_id=1, replica_groups={{0,1,2,3,4,5,6,7,16,17,18,19,20,21,22,23,32,33,34,35,36,37,38,39,48,49,..., dimensions={0} | all-to-all | bytes 9961472 | tf_op jit(solution)/shard_map/all_to_all | solution.py:266
  78.0 0.0 copy-start.5
  78.0 0.4 slice.8
  78.4 1.8 %copy-done.5 = bf16[64,304,128]{2,1,0:T(8,128)(2,1)} copy-done((bf16[64,304,128]{2,1,0:T(8,128)(2,1)}, bf16[64,304,128]{2,1,0:T(8,128)(2,1)S(1)}, u32[]{:S(2)}) %copy-start.5) | copy-done | bytes 4980760
  80.2 2.5 %collective-permute-start = (bf16[64,192,128]{2,1,0:T(8,128)(2,1)S(1)}, bf16[64,192,128]{2,1,0:T(8,128)(2,1)S(1)}, u32[]{:S(2)}, u32[]{:S(2)}) collective-permute-start(bf16[64,192,128]{2,1,0:T(8,128)(2,1)S(1)} %slice.8), channel_id=1, source_target_pairs={{0,8},{8,0},{16,24},{24,16},{32,40},{40,32},{48,56},{56,48},{64,72... | collective-permute-start | bytes 9437192 | tf_op jit(solution)/shard_map/ppermute | solution.py:270
  82.7 5.3 %collective-permute-done.sib_hbm = bf16[64,192,128]{2,1,0:T(8,128)(2,1)S(1)} collective-permute-done((bf16[64,192,128]{2,1,0:T(8,128)(2,1)S(1)}, bf16[64,192,128]{2,1,0:T(8,128)(2,1)S(1)}, u32[]{:S(2)}, u32[]{:S(2)}) %collective-permute-start) | collective-permute-done | bytes 3145760 | tf_op jit(solution)/shard_map/ppermute | solution.py:270
  88.0 21.5 %attend.1 = bf16[64,96,128]{2,1,0:T(8,128)(2,1)S(1)} custom-call(bf16[64,304,128]{2,1,0:T(8,128)(2,1)} %copy-done.5, bf16[64,192,128]{2,1,0:T(8,128)(2,1)S(1)} %collective-permute-done.sib_hbm), custom_call_target="tpu_custom_call" | custom-call | flops 4831838208 | bytes 12582912 | tf_op jit(solution)/shard_map/attend/pallas_call | solution.py:207
  109.5 28.5 %all_to_all.11 = bf16[64,96,128]{2,1,0:T(8,128)(2,1)S(1)} all-to-all(bf16[64,96,128]{2,1,0:T(8,128)(2,1)S(1)} %attend.1), channel_id=1, replica_groups={{0,1,2,3,4,5,6,7,16,17,18,19,20,21,22,23,32,33,34,35,36,37,38,39,48,49,..., dimensions={0} | all-to-all | bytes 3145728 | tf_op jit(solution)/shard_map/all_to_all | solution.py:274
  137.9 1.0 copy_bitcast_fusion
Async XLA Ops:
  0.0 1.2 copy-start
  1.2 1.2 copy-start.1
  2.4 1.2 copy-start.2
  3.6 0.7 copy-start.3
  4.3 0.7 copy-start.4
  78.0 2.2 %copy-start.5 = (bf16[64,304,128]{2,1,0:T(8,128)(2,1)}, bf16[64,304,128]{2,1,0:T(8,128)(2,1)S(1)}, u32[]{:S(2)}) copy-start(bf16[64,304,128]{2,1,0:T(8,128)(2,1)S(1)} %all_to_all.10.own_hbm) | copy-start | bytes 14942212
  80.2 7.8 %collective-permute-start = (bf16[64,192,128]{2,1,0:T(8,128)(2,1)S(1)}, bf16[64,192,128]{2,1,0:T(8,128)(2,1)S(1)}, u32[]{:S(2)}, u32[]{:S(2)}) collective-permute-start(bf16[64,192,128]{2,1,0:T(8,128)(2,1)S(1)} %slice.8), channel_id=1, source_target_pairs={{0,8},{8,0},{16,24},{24,16},{32,40},{40,32},{48,56},{56,48},{64,72... | collective-permute-start | bytes 9437192 | tf_op jit(solution)/shard_map/ppermute | solution.py:270

commit v6 on v5

v6 whole, which is shorter than its diff:
```python
import functools
import math

import jax
import jax.numpy as jnp
from jax import lax
from jax.experimental import pallas as pl
from jax.experimental.pallas import tpu as pltpu
from jax.sharding import PartitionSpec as P

HEAD_DIM = 128
MAXK = 4
CORES = 2
TABLE_ROWS = 16
PACK_STEPS = 2
MIB = 1 << 20


def pack_kernel(q_ref, k_ref, v_ref, pairs_ref, count_ref, o_ref, table):
    tokens, width = q_ref.shape
    row_tiles = pairs_ref.shape[0]
    table[...] = jnp.zeros_like(table)
    table[pl.ds(0, row_tiles), pl.ds(0, MAXK)] = pairs_ref[...].astype(jnp.float32)
    table[pl.ds(row_tiles, 1), pl.ds(0, row_tiles)] = count_ref[...].astype(jnp.float32)
    for h in range(width // HEAD_DIM):
        cols = pl.ds(h * HEAD_DIM, HEAD_DIM)
        for part, ref in enumerate((k_ref, v_ref, q_ref)):
            o_ref[h, pl.ds(part * tokens, tokens), :] = ref[:, cols]
        o_ref[h, pl.ds(3 * tokens, TABLE_ROWS), :] = table[...].astype(jnp.bfloat16)


def attend_kernel(own, sib, outs, *scratch, row_len, row_tiles):
    kv, scores, peaks, totals, rows_int, table, place, order, table_sem = scratch
    chips, tokens, _ = outs.shape
    sources = row_len // row_tiles
    tile_len = sources * tokens
    tiles = chips // sources
    core = lax.axis_index("seq") % CORES
    factor = math.log2(math.e) / math.sqrt(HEAD_DIM)

    for row in range(chips // row_len):
        block = own[row * row_len, pl.ds(3 * tokens, TABLE_ROWS), :].astype(jnp.float32)
        rows_int[row] = block[: rows_int.shape[1]].astype(jnp.int32)
    spread = pltpu.make_async_copy(rows_int, table, table_sem.at[0])
    spread.start()

    def gather(source, carry):
        kv[source] = own[source, pl.ds(0, 2 * tokens), :]
        kv[chips + source] = sib[source]
        return carry

    lax.fori_loop(0, chips, gather, 0)
    spread.wait()

    def sort(local, filled):
        at, w = local // row_tiles, local % row_tiles
        for m in range(MAXK):
            tile = jnp.clip(table[at, w, m], 0, CORES * tiles - 1)
            row = tile // row_tiles
            side = (row + core) % CORES
            place[local, m] = side * chips + row // CORES * row_len + tile % row_tiles * sources
        full = table[at, row_tiles, w] > MAXK - 1
        n_full, n_less = filled

        @pl.when(full)
        def _():
            order[0, n_full] = local

        @pl.when(jnp.logical_not(full))
        def _():
            order[1, n_less] = local

        step = full.astype(jnp.int32)
        return n_full + step, n_less + 1 - step

    filled = lax.fori_loop(0, tiles, sort, (jnp.int32(0), jnp.int32(0)))

    def listed(local, m, part):
        block = kv[pl.ds(place[local, m], sources), pl.ds(part * tokens, tokens), :]
        return block.reshape(tile_len, HEAD_DIM)

    def query_of(local):
        block = own[pl.ds(local * sources, sources), pl.ds(2 * tokens, tokens), :]
        return block.reshape(tile_len, HEAD_DIM)

    def score(local, m, query, peak):
        block = lax.dot_general(
            query, listed(local, m, 0), (((1,), (1,)), ((), ())), preferred_element_type=jnp.float32
        )
        scores[m] = block
        for at in range(0, tile_len, HEAD_DIM):
            part = block[:, at : at + HEAD_DIM]
            peak = part if peak is None else jnp.maximum(peak, part)
        return peak

    def weigh(local, m, peak, total):
        probs = jnp.exp2((scores[m] - peak) * factor).astype(jnp.bfloat16)
        value = listed(local, m, 1)
        value = jnp.concatenate([value, jnp.ones_like(value)], axis=1)
        return total + jnp.dot(probs, value, preferred_element_type=jnp.float32)

    def finish(local):
        out = totals[:, :HEAD_DIM] / totals[:, HEAD_DIM:]
        outs[pl.ds(local * sources, sources)] = out.astype(outs.dtype).reshape(
            sources, tokens, HEAD_DIM
        )

    def pair(before, this, then, count):
        query = query_of(then)
        finish(before)
        peak = jnp.max(peaks[...], axis=-1, keepdims=True)
        peak = jnp.broadcast_to(peak, (tile_len, tile_len))
        total = jnp.zeros((tile_len, 2 * HEAD_DIM), jnp.float32)
        then_peak = None
        for m in range(count):
            total = weigh(this, m, peak, total)
            then_peak = score(then, m, query, then_peak)
        peaks[...] = then_peak
        totals[...] = total

    for kind, count in enumerate((MAXK, MAXK - 1)):
        number = filled[kind]

        def pick(i, kind=kind, number=number):
            return order[kind, jnp.minimum(i, number - 1)]

        def first(count=count, pick=pick):
            local = pick(0)
            query, peak = query_of(local), None
            for m in range(count):
                peak = score(local, m, query, peak)
            peaks[...] = peak

        pl.when(number > 0)(first)

        def step(i, carry, count=count, pick=pick):
            pair(pick(jnp.maximum(i - 1, 0)), pick(i), pick(i + 1), count)
            return carry

        lax.fori_loop(0, number, step, 0)
        pl.when(number > 0)(lambda pick=pick, number=number: finish(pick(number - 1)))


def attend_call(own, sib, *, row_len, row_tiles):
    chips, tokens = own.shape[0], sib.shape[1] // 2
    sources = row_len // row_tiles
    tiles = chips // sources
    tile_len = sources * tokens
    flops = 4 * tiles * tile_len * MAXK * tile_len * HEAD_DIM
    vmem = pl.BlockSpec(memory_space=pltpu.VMEM)
    return pl.pallas_call(
        functools.partial(attend_kernel, row_len=row_len, row_tiles=row_tiles),
        in_specs=[vmem, vmem],
        out_specs=vmem,
        scratch_shapes=[
            pltpu.VMEM((CORES * chips, 2 * tokens, HEAD_DIM), jnp.bfloat16),
            pltpu.VMEM((MAXK, tile_len, tile_len), jnp.float32),
            pltpu.VMEM((tile_len, HEAD_DIM), jnp.float32),
            pltpu.VMEM((tile_len, 2 * HEAD_DIM), jnp.float32),
            pltpu.VMEM((chips // row_len, 8, HEAD_DIM), jnp.int32),
            pltpu.SMEM((chips // row_len, 8, HEAD_DIM), jnp.int32),
            pltpu.SMEM((tiles, MAXK), jnp.int32),
            pltpu.SMEM((2, tiles), jnp.int32),
            pltpu.SemaphoreType.DMA((1,)),
        ],
        out_shape=jax.ShapeDtypeStruct((chips, tokens, HEAD_DIM), jnp.bfloat16),
        compiler_params=pltpu.CompilerParams(vmem_limit_bytes=24 * MIB),
        cost_estimate=pl.CostEstimate(
            flops=flops, bytes_accessed=12 * MIB, transcendentals=flops // (4 * HEAD_DIM)
        ),
        name="attend",
    )(own, sib)


def local(queries, keys, values, pairs, pair_count):
    axes = ("seq", "head")
    rows_all = lax.axis_size("seq")
    head_size = lax.axis_size("head")
    tokens, width = queries.shape
    heads = width // HEAD_DIM
    row_tiles = pairs.shape[0]
    chips = rows_all * head_size // CORES
    slot = 3 * tokens + TABLE_ROWS
    same_core = [
        [s * head_size + h for s in range(core, rows_all, CORES) for h in range(head_size)]
        for core in range(CORES)
    ]

    some = heads // PACK_STEPS
    packed = pl.pallas_call(
        pack_kernel,
        grid=(PACK_STEPS,),
        in_specs=[pl.BlockSpec((tokens, some * HEAD_DIM), lambda i: (0, i))] * 3
        + [
            pl.BlockSpec((row_tiles, MAXK), lambda i: (0, 0)),
            pl.BlockSpec((1, row_tiles), lambda i: (0, 0)),
        ],
        out_specs=pl.BlockSpec((some, slot, HEAD_DIM), lambda i: (i, 0, 0)),
        out_shape=jax.ShapeDtypeStruct((chips, slot, HEAD_DIM), jnp.bfloat16),
        scratch_shapes=[pltpu.VMEM((TABLE_ROWS, HEAD_DIM), jnp.float32)],
        compiler_params=pltpu.CompilerParams(vmem_limit_bytes=56 * MIB),
        name="pack",
    )(queries, keys, values, pairs, pair_count.reshape(1, row_tiles))
    own = lax.all_to_all(
        packed, axes, split_axis=0, concat_axis=0, tiled=True, axis_index_groups=same_core
    )
    swap = [(s, s ^ 1) for s in range(rows_all)]
    sib = lax.ppermute(own[:, : 2 * tokens], "seq", swap)
    attended = attend_call(own, sib, row_len=head_size, row_tiles=row_tiles)
    back = lax.all_to_all(
        attended, axes, split_axis=0, concat_axis=0, tiled=True, axis_index_groups=same_core
    )
    return back[:heads].transpose(1, 0, 2).reshape(tokens, width)


def solution(mesh):
    placed = (
        P(("seq", "head"), None),
        P(("seq", "head"), None),
        P(("seq", "head"), None),
        P("seq", None),
        P("seq"),
    )
    return jax.shard_map(
        local, mesh=mesh, in_specs=placed, out_specs=P(("seq", "head"), None), check_vma=False
    )
```

time: 139 us -> 129 us (0.928); the launches traced: 139 us -> 127 us
  local copies, waits for them, and re-layouts: 8.18 us -> 1.43 us
  Pallas kernels: 23.4 us -> 19.6 us
    unnamed x12 -> x0, local copies, waits for them, and re-layouts: 6.75 us -> none
    pallas_call x1, Pallas kernels: 21.5 us -> 16.3 us  [attend_call(): pl.pallas_call(functools.partial(attend_kernel, row_len=row_len, row_tile...]
where the time goes in v6:
time: 129 us; the launch traced here: 127 us
  blocking collectives  98.4 us (76%)
  Pallas kernels  19.6 us (15%)
  waiting for transfers between devices  5.29 us (4%)
  starting transfers between devices  2.59 us (2%)
  local copies, waits for them, and re-layouts  1.43 us (1%)
    all_to_all x1, blocking collectives, local(): lax.all_to_all(packed, axes, split_axis=0, concat_axis=0, tiled=True, axi...  71.3 us
    all_to_all x1, blocking collectives, local(): lax.all_to_all(attended, axes, split_axis=0, concat_axis=0, tiled=True, a...  27.1 us
    pallas_call x1, Pallas kernels, attend_call(): pl.pallas_call(functools.partial(attend_kernel, row_len=row_len, row_tile...  16.3 us
    ppermute x1, waiting for transfers between devices, local(): sib = lax.ppermute(own[:, :2 * tokens], 'seq', swap)  5.29 us
    pallas_call x1, Pallas kernels, local(): pl.pallas_call(pack_kernel, grid=(PACK_STEPS,), in_specs=[pl.BlockSpec((t...  3.25 us
    ppermute x1, starting transfers between devices, local(): sib = lax.ppermute(own[:, :2 * tokens], 'seq', swap)  2.59 us
  transfers between devices with their start and end apart: 1, of which 1 were waited for; matrix products, arithmetic and copies ran while one was open for 0% of the time, Pallas kernels for 0%

profile of v6, /device:TPU:1, one launch (start us, length us, event | category | flops | bytes accessed | tf_op | source)
XLA Modules:
  0.0 127.3 jit_solution(8717402583798460666)
XLA Ops:
  0.0 3.3 %pack.1 = bf16[64,304,128]{2,1,0:T(8,128)(2,1)} custom-call(bf16[96,5120]{1,0:T(8,128)(2,1)} %q_ref.1, bf16[96,5120]{1,0:T(8,128)(2,1)} %k_ref.1, bf16[96,5120]{1,0:T(8,128)(2,1)} %v_ref.1, s32[2,4]{1,0:T(2,128)} %pairs_ref.1, s32[1,2]{1,0:T(1,128)} %bitcast.7), custom_call_target="tpu_custom_call" | custom-call | tf_op jit(solution)/shard_map/pack/pallas_call | solution.py:190
  3.3 71.3 %all_to_all.10.own = bf16[64,304,128]{2,1,0:T(8,128)(2,1)S(1)} all-to-all(bf16[64,304,128]{2,1,0:T(8,128)(2,1)} %pack.1), channel_id=1, replica_groups={{0,1,2,3,4,5,6,7,16,17,18,19,20,21,22,23,32,33,34,35,36,37,38,39,48,49,..., dimensions={0} | all-to-all | bytes 9961472 | tf_op jit(solution)/shard_map/all_to_all | solution.py:204
  74.5 0.4 slice.8
  74.9 2.6 %collective-permute-start = (bf16[64,192,128]{2,1,0:T(8,128)(2,1)S(1)}, bf16[64,192,128]{2,1,0:T(8,128)(2,1)S(1)}, u32[]{:S(2)}, u32[]{:S(2)}) collective-permute-start(bf16[64,192,128]{2,1,0:T(8,128)(2,1)S(1)} %slice.8), channel_id=1, source_target_pairs={{0,8},{8,0},{16,24},{24,16},{32,40},{40,32},{48,56},{56,48},{64,72... | collective-permute-start | bytes 9437192 | tf_op jit(solution)/shard_map/ppermute | solution.py:208
  77.5 5.3 %collective-permute-done.sib = bf16[64,192,128]{2,1,0:T(8,128)(2,1)S(1)} collective-permute-done((bf16[64,192,128]{2,1,0:T(8,128)(2,1)S(1)}, bf16[64,192,128]{2,1,0:T(8,128)(2,1)S(1)}, u32[]{:S(2)}, u32[]{:S(2)}) %collective-permute-start) | collective-permute-done | bytes 3145760 | tf_op jit(solution)/shard_map/ppermute | solution.py:208
  82.8 16.3 %attend.1 = bf16[64,96,128]{2,1,0:T(8,128)(2,1)S(1)} custom-call(bf16[64,304,128]{2,1,0:T(8,128)(2,1)S(1)} %all_to_all.10.own, bf16[64,192,128]{2,1,0:T(8,128)(2,1)S(1)} %collective-permute-done.sib), custom_call_target="tpu_custom_call" | custom-call | flops 4831838208 | bytes 12582912 | tf_op jit(solution)/shard_map/attend/pallas_call | solution.py:151
  99.1 27.1 %all_to_all.11 = bf16[64,96,128]{2,1,0:T(8,128)(2,1)S(1)} all-to-all(bf16[64,96,128]{2,1,0:T(8,128)(2,1)S(1)} %attend.1), channel_id=1, replica_groups={{0,1,2,3,4,5,6,7,16,17,18,19,20,21,22,23,32,33,34,35,36,37,38,39,48,49,..., dimensions={0} | all-to-all | bytes 3145728 | tf_op jit(solution)/shard_map/all_to_all | solution.py:210
  126.3 1.0 copy_bitcast_fusion
Async XLA Ops:
  74.9 7.9 %collective-permute-start = (bf16[64,192,128]{2,1,0:T(8,128)(2,1)S(1)}, bf16[64,192,128]{2,1,0:T(8,128)(2,1)S(1)}, u32[]{:S(2)}, u32[]{:S(2)}) collective-permute-start(bf16[64,192,128]{2,1,0:T(8,128)(2,1)S(1)} %slice.8), channel_id=1, source_target_pairs={{0,8},{8,0},{16,24},{24,16},{32,40},{40,32},{48,56},{56,48},{64,72... | collective-permute-start | bytes 9437192 | tf_op jit(solution)/shard_map/ppermute | solution.py:208

commit v7 on v6

--- a/solution.py
+++ b/solution.py
@@ -13,6 +13,7 @@
 CORES = 2
 TABLE_ROWS = 16
 PACK_STEPS = 2
+SELF_UNROLL = 2
 MIB = 1 << 20
 
 
@@ -29,7 +30,43 @@
         o_ref[h, pl.ds(3 * tokens, TABLE_ROWS), :] = table[...].astype(jnp.bfloat16)
 
 
-def attend_kernel(own, sib, outs, *scratch, row_len, row_tiles):
+def rows_of(ref, first, sources, part, tokens):
+    block = ref[pl.ds(first, sources), pl.ds(part * tokens, tokens), :]
+    return block.reshape(sources * tokens, HEAD_DIM)
+
+
+def product(query, key):
+    return lax.dot_general(
+        query, key, (((1,), (1,)), ((), ())), preferred_element_type=jnp.float32
+    )
+
+
+def with_ones(value):
+    return jnp.concatenate([value, jnp.ones_like(value)], axis=1)
+
+
+def self_kernel(own, totals, peaks, *, sources, tokens):
+    tile_len = sources * tokens
+    factor = math.log2(math.e) / math.sqrt(HEAD_DIM)
+
+    def step(i, carry):
+        tiles = [i * SELF_UNROLL + u for u in range(SELF_UNROLL)]
+        key, value, query = (
+            [rows_of(own, tile * sources, sources, part, tokens) for tile in tiles]
+            for part in range(3)
+        )
+        scores = [product(q, k) for q, k in zip(query, key)]
+        for tile, block, v in zip(tiles, scores, value):
+            peak = jnp.max(block, axis=-1, keepdims=True)
+            probs = jnp.exp2((block - peak) * factor).astype(jnp.bfloat16)
+            totals[tile] = jnp.dot(probs, with_ones(v), preferred_element_type=jnp.float32)
+            peaks[tile] = jnp.broadcast_to(peak, (tile_len, HEAD_DIM))
+        return carry
+
+    lax.fori_loop(0, peaks.shape[0] // SELF_UNROLL, step, 0)
+
+
+def attend_kernel(own, sib, base_totals, base_peaks, outs, *scratch, row_len, row_tiles):
     kv, scores, peaks, totals, rows_int, table, place, order, table_sem = scratch
     chips, tokens, _ = outs.shape
     sources = row_len // row_tiles
@@ -76,27 +113,21 @@
     filled = lax.fori_loop(0, tiles, sort, (jnp.int32(0), jnp.int32(0)))
 
     def listed(local, m, part):
-        block = kv[pl.ds(place[local, m], sources), pl.ds(part * tokens, tokens), :]
-        return block.reshape(tile_len, HEAD_DIM)
+        return rows_of(kv, place[local, m], sources, part, tokens)
 
     def query_of(local):
-        block = own[pl.ds(local * sources, sources), pl.ds(2 * tokens, tokens), :]
-        return block.reshape(tile_len, HEAD_DIM)
+        return rows_of(own, local * sources, sources, 2, tokens)
 
     def score(local, m, query, peak):
-        block = lax.dot_general(
-            query, listed(local, m, 0), (((1,), (1,)), ((), ())), preferred_element_type=jnp.float32
-        )
-        scores[m] = block
+        block = product(query, listed(local, m, 0))
+        scores[m - 1] = block
         for at in range(0, tile_len, HEAD_DIM):
-            part = block[:, at : at + HEAD_DIM]
-            peak = part if peak is None else jnp.maximum(peak, part)
+            peak = jnp.maximum(peak, block[:, at : at + HEAD_DIM])
         return peak
 
     def weigh(local, m, peak, total):
-        probs = jnp.exp2((scores[m] - peak) * factor).astype(jnp.bfloat16)
-        value = listed(local, m, 1)
-        value = jnp.concatenate([value, jnp.ones_like(value)], axis=1)
+        probs = jnp.exp2((scores[m - 1] - peak) * factor).astype(jnp.bfloat16)
+        value = with_ones(listed(local, m, 1))
         return total + jnp.dot(probs, value, preferred_element_type=jnp.float32)
 
     def finish(local):
@@ -109,10 +140,11 @@
         query = query_of(then)
         finish(before)
         peak = jnp.max(peaks[...], axis=-1, keepdims=True)
+        scale = jnp.exp2((base_peaks[this] - peak) * factor)
+        total = base_totals[this] * jnp.concatenate([scale, scale], axis=1)
         peak = jnp.broadcast_to(peak, (tile_len, tile_len))
-        total = jnp.zeros((tile_len, 2 * HEAD_DIM), jnp.float32)
-        then_peak = None
-        for m in range(count):
+        then_peak = base_peaks[then]
+        for m in range(1, count):
             total = weigh(this, m, peak, total)
             then_peak = score(then, m, query, then_peak)
         peaks[...] = then_peak
@@ -126,8 +158,8 @@
 
         def first(count=count, pick=pick):
             local = pick(0)
-            query, peak = query_of(local), None
-            for m in range(count):
+            query, peak = query_of(local), base_peaks[local]
+            for m in range(1, count):
                 peak = score(local, m, query, peak)
             peaks[...] = peak
 
@@ -141,20 +173,39 @@
         pl.when(number > 0)(lambda pick=pick, number=number: finish(pick(number - 1)))
 
 
-def attend_call(own, sib, *, row_len, row_tiles):
+def self_call(own, *, tokens, sources):
+    tiles, tile_len = own.shape[0] // sources, sources * tokens
+    flops = 4 * tiles * tile_len * tile_len * HEAD_DIM
+    vmem = pl.BlockSpec(memory_space=pltpu.VMEM)
+    return pl.pallas_call(
+        functools.partial(self_kernel, sources=sources, tokens=tokens),
+        in_specs=[vmem],
+        out_specs=[vmem, vmem],
+        out_shape=[
+            jax.ShapeDtypeStruct((tiles, tile_len, 2 * HEAD_DIM), jnp.float32),
+            jax.ShapeDtypeStruct((tiles, tile_len, HEAD_DIM), jnp.float32),
+        ],
+        compiler_params=pltpu.CompilerParams(vmem_limit_bytes=24 * MIB),
+        cost_estimate=pl.CostEstimate(
+            flops=flops, bytes_accessed=12 * MIB, transcendentals=flops // (4 * HEAD_DIM)
+        ),
+        name="attend_self",
+    )(own)
+
+
+def attend_call(own, sib, totals, peaks, *, row_len, row_tiles):
     chips, tokens = own.shape[0], sib.shape[1] // 2
     sources = row_len // row_tiles
-    tiles = chips // sources
-    tile_len = sources * tokens
-    flops = 4 * tiles * tile_len * MAXK * tile_len * HEAD_DIM
+    tiles, tile_len, _ = peaks.shape
+    flops = 4 * tiles * tile_len * (MAXK - 1) * tile_len * HEAD_DIM
     vmem = pl.BlockSpec(memory_space=pltpu.VMEM)
     return pl.pallas_call(
         functools.partial(attend_kernel, row_len=row_len, row_tiles=row_tiles),
-        in_specs=[vmem, vmem],
+        in_specs=[vmem] * 4,
         out_specs=vmem,
         scratch_shapes=[
             pltpu.VMEM((CORES * chips, 2 * tokens, HEAD_DIM), jnp.bfloat16),
-            pltpu.VMEM((MAXK, tile_len, tile_len), jnp.float32),
+            pltpu.VMEM((MAXK - 1, tile_len, tile_len), jnp.float32),
             pltpu.VMEM((tile_len, HEAD_DIM), jnp.float32),
             pltpu.VMEM((tile_len, 2 * HEAD_DIM), jnp.float32),
             pltpu.VMEM((chips // row_len, 8, HEAD_DIM), jnp.int32),
@@ -169,7 +220,7 @@
             flops=flops, bytes_accessed=12 * MIB, transcendentals=flops // (4 * HEAD_DIM)
         ),
         name="attend",
-    )(own, sib)
+    )(own, sib, totals, peaks)
 
 
 def local(queries, keys, values, pairs, pair_count):
@@ -206,7 +257,8 @@
     )
     swap = [(s, s ^ 1) for s in range(rows_all)]
     sib = lax.ppermute(own[:, : 2 * tokens], "seq", swap)
-    attended = attend_call(own, sib, row_len=head_size, row_tiles=row_tiles)
+    totals, peaks = self_call(own, tokens=tokens, sources=head_size // row_tiles)
+    attended = attend_call(own, sib, totals, peaks, row_len=head_size, row_tiles=row_tiles)
     back = lax.all_to_all(
         attended, axes, split_axis=0, concat_axis=0, tiled=True, axis_index_groups=same_core
     )

time: 129 us -> 128 us (level); the launches traced: 127 us -> 128 us
  waiting for transfers between devices: 5.29 us -> 0.01 us
  Pallas kernels: 19.6 us -> 23.6 us
  blocking collectives: 98.4 us -> 101 us
    pallas_call x0 -> x1, Pallas kernels: none -> 5.86 us  [self_call(): pl.pallas_call(functools.partial(self_kernel, sources=sources, tokens=tok...]
    ppermute x1, waiting for transfers between devices: 5.29 us -> 0.01 us  [local(): sib = lax.ppermute(own[:, :2 * tokens], 'seq', swap)]
    all_to_all x1, blocking collectives: 27.1 us -> 29.3 us  [local(): lax.all_to_all(attended, axes, split_axis=0, concat_axis=0, tiled=True, a...]
    pallas_call x1, Pallas kernels: 16.3 us -> 14.5 us  [attend_call(): pl.pallas_call(functools.partial(attend_kernel, row_len=row_len, row_tile...]
  transfers between devices with their start and end apart: 1 -> 1, of which waited for: 1 -> 0; matrix products, arithmetic and copies ran while one was open for 0% -> 0% of each run, Pallas kernels for 0% -> 5%
where the time goes in v7:
time: 128 us
  blocking collectives  101 us (79%)
  Pallas kernels  23.6 us (18%)
  starting transfers between devices  2.59 us (2%)
  local copies, waits for them, and re-layouts  1.43 us (1%)
    all_to_all x1, blocking collectives, local(): lax.all_to_all(packed, axes, split_axis=0, concat_axis=0, tiled=True, axi...  71.3 us
    all_to_all x1, blocking collectives, local(): lax.all_to_all(attended, axes, split_axis=0, concat_axis=0, tiled=True, a...  29.3 us
    pallas_call x1, Pallas kernels, attend_call(): pl.pallas_call(functools.partial(attend_kernel, row_len=row_len, row_tile...  14.5 us
    pallas_call x1, Pallas kernels, self_call(): pl.pallas_call(functools.partial(self_kernel, sources=sources, tokens=tok...  5.86 us
    pallas_call x1, Pallas kernels, local(): pl.pallas_call(pack_kernel, grid=(PACK_STEPS,), in_specs=[pl.BlockSpec((t...  3.25 us
    ppermute x1, starting transfers between devices, local(): sib = lax.ppermute(own[:, :2 * tokens], 'seq', swap)  2.59 us
  transfers between devices with their start and end apart: 1, of which 0 were waited for; matrix products, arithmetic and copies ran while one was open for 0% of the time, Pallas kernels for 5%

profile of v7, /device:TPU:1, one launch (start us, length us, event | category | flops | bytes accessed | tf_op | source)
XLA Modules:
  0.0 128.2 jit_solution(1529240191952167720)
XLA Ops:
  0.0 3.2 %pack.1 = bf16[64,304,128]{2,1,0:T(8,128)(2,1)} custom-call(bf16[96,5120]{1,0:T(8,128)(2,1)} %q_ref.1, bf16[96,5120]{1,0:T(8,128)(2,1)} %k_ref.1, bf16[96,5120]{1,0:T(8,128)(2,1)} %v_ref.1, s32[2,4]{1,0:T(2,128)} %pairs_ref.1, s32[1,2]{1,0:T(1,128)} %bitcast.7), custom_call_target="tpu_custom_call" | custom-call | tf_op jit(solution)/shard_map/pack/pallas_call | solution.py:241
  3.3 71.3 %all_to_all.10.own = bf16[64,304,128]{2,1,0:T(8,128)(2,1)S(1)} all-to-all(bf16[64,304,128]{2,1,0:T(8,128)(2,1)} %pack.1), channel_id=1, replica_groups={{0,1,2,3,4,5,6,7,16,17,18,19,20,21,22,23,32,33,34,35,36,37,38,39,48,49,..., dimensions={0} | all-to-all | bytes 9961472 | tf_op jit(solution)/shard_map/all_to_all | solution.py:255
  74.5 0.4 slice.8
  74.9 2.6 %collective-permute-start = (bf16[64,192,128]{2,1,0:T(8,128)(2,1)S(1)}, bf16[64,192,128]{2,1,0:T(8,128)(2,1)S(1)}, u32[]{:S(2)}, u32[]{:S(2)}) collective-permute-start(bf16[64,192,128]{2,1,0:T(8,128)(2,1)S(1)} %slice.8), channel_id=1, source_target_pairs={{0,8},{8,0},{16,24},{24,16},{32,40},{40,32},{48,56},{56,48},{64,72... | collective-permute-start | bytes 9437192 | tf_op jit(solution)/shard_map/ppermute | solution.py:259
  77.5 5.9 %attend_self.1 = (f32[16,384,256]{2,1,0:T(8,128)S(1)}, f32[16,384,128]{2,1,0:T(8,128)S(1)}) custom-call(bf16[64,304,128]{2,1,0:T(8,128)(2,1)S(1)} %all_to_all.10.own), custom_call_target="tpu_custom_call" | custom-call | flops 1207959552 | bytes 12582912 | tf_op jit(solution)/shard_map/attend_self/pallas_call | solution.py:180
  83.4 0.0 collective-permute-done.sib
  83.4 14.5 %attend.1 = bf16[64,96,128]{2,1,0:T(8,128)(2,1)S(1)} custom-call(bf16[64,304,128]{2,1,0:T(8,128)(2,1)S(1)} %all_to_all.10.own, bf16[64,192,128]{2,1,0:T(8,128)(2,1)S(1)} %collective-permute-done.sib, f32[16,384,256]{2,1,0:T(8,128)S(1)} %get-tuple-element.7.base_totals, f32[16,384,128]{2,1,0:T(8,128)S(1)} %get-tuple-element.8.base_peaks), custom_call_target="tpu_custom_call" | custom-call | flops 3623878656 | bytes 12582912 | tf_op jit(solution)/shard_map/attend/pallas_call | solution.py:202
  97.8 29.3 %all_to_all.11 = bf16[64,96,128]{2,1,0:T(8,128)(2,1)S(1)} all-to-all(bf16[64,96,128]{2,1,0:T(8,128)(2,1)S(1)} %attend.1), channel_id=1, replica_groups={{0,1,2,3,4,5,6,7,16,17,18,19,20,21,22,23,32,33,34,35,36,37,38,39,48,49,..., dimensions={0} | all-to-all | bytes 3145728 | tf_op jit(solution)/shard_map/all_to_all | solution.py:262
  127.1 1.0 copy_bitcast_fusion
Async XLA Ops:
  74.9 8.5 %collective-permute-start = (bf16[64,192,128]{2,1,0:T(8,128)(2,1)S(1)}, bf16[64,192,128]{2,1,0:T(8,128)(2,1)S(1)}, u32[]{:S(2)}, u32[]{:S(2)}) collective-permute-start(bf16[64,192,128]{2,1,0:T(8,128)(2,1)S(1)} %slice.8), channel_id=1, source_target_pairs={{0,8},{8,0},{16,24},{24,16},{32,40},{40,32},{48,56},{56,48},{64,72... | collective-permute-start | bytes 9437192 | tf_op jit(solution)/shard_map/ppermute | solution.py:259

commit v8 on v7

--- a/solution.py
+++ b/solution.py
@@ -13,7 +13,8 @@
 CORES = 2
 TABLE_ROWS = 16
 PACK_STEPS = 2
-SELF_UNROLL = 2
+SELF_UNROLL = 4
+ORDER, FILLED = MAXK, MAXK + 2
 MIB = 1 << 20
 
 
@@ -45,75 +46,75 @@
     return jnp.concatenate([value, jnp.ones_like(value)], axis=1)
 
 
-def self_kernel(own, totals, peaks, *, sources, tokens):
+def self_kernel(own, totals, peaks, info, rows_int, table, table_sem, *, row_len, row_tiles):
+    chips, tokens = own.shape[0], (own.shape[1] - TABLE_ROWS) // 3
+    sources = row_len // row_tiles
     tile_len = sources * tokens
+    tiles = chips // sources
+    core = lax.axis_index("seq") % CORES
     factor = math.log2(math.e) / math.sqrt(HEAD_DIM)
 
+    for row in range(chips // row_len):
+        block = own[row * row_len, pl.ds(3 * tokens, TABLE_ROWS), :].astype(jnp.float32)
+        rows_int[row] = block[: rows_int.shape[1]].astype(jnp.int32)
+    spread = pltpu.make_async_copy(rows_int, table, table_sem.at[0])
+    spread.start()
+
     def step(i, carry):
-        tiles = [i * SELF_UNROLL + u for u in range(SELF_UNROLL)]
+        some = [i * SELF_UNROLL + u for u in range(SELF_UNROLL)]
         key, value, query = (
-            [rows_of(own, tile * sources, sources, part, tokens) for tile in tiles]
+            [rows_of(own, tile * sources, sources, part, tokens) for tile in some]
             for part in range(3)
         )
         scores = [product(q, k) for q, k in zip(query, key)]
-        for tile, block, v in zip(tiles, scores, value):
+        for tile, block, v in zip(some, scores, value):
             peak = jnp.max(block, axis=-1, keepdims=True)
             probs = jnp.exp2((block - peak) * factor).astype(jnp.bfloat16)
             totals[tile] = jnp.dot(probs, with_ones(v), preferred_element_type=jnp.float32)
             peaks[tile] = jnp.broadcast_to(peak, (tile_len, HEAD_DIM))
         return carry
 
-    lax.fori_loop(0, peaks.shape[0] // SELF_UNROLL, step, 0)
-
-
-def attend_kernel(own, sib, base_totals, base_peaks, outs, *scratch, row_len, row_tiles):
-    kv, scores, peaks, totals, rows_int, table, place, order, table_sem = scratch
-    chips, tokens, _ = outs.shape
-    sources = row_len // row_tiles
-    tile_len = sources * tokens
-    tiles = chips // sources
-    core = lax.axis_index("seq") % CORES
-    factor = math.log2(math.e) / math.sqrt(HEAD_DIM)
-
-    for row in range(chips // row_len):
-        block = own[row * row_len, pl.ds(3 * tokens, TABLE_ROWS), :].astype(jnp.float32)
-        rows_int[row] = block[: rows_int.shape[1]].astype(jnp.int32)
-    spread = pltpu.make_async_copy(rows_int, table, table_sem.at[0])
-    spread.start()
-
-    def gather(source, carry):
-        kv[source] = own[source, pl.ds(0, 2 * tokens), :]
-        kv[chips + source] = sib[source]
-        return carry
-
-    lax.fori_loop(0, chips, gather, 0)
+    lax.fori_loop(0, tiles // SELF_UNROLL, step, 0)
     spread.wait()
 
     def sort(local, filled):
         at, w = local // row_tiles, local % row_tiles
-        for m in range(MAXK):
+        for m in range(1, MAXK):
             tile = jnp.clip(table[at, w, m], 0, CORES * tiles - 1)
             row = tile // row_tiles
             side = (row + core) % CORES
-            place[local, m] = side * chips + row // CORES * row_len + tile % row_tiles * sources
+            info[local, m] = side * chips + row // CORES * row_len + tile % row_tiles * sources
         full = table[at, row_tiles, w] > MAXK - 1
         n_full, n_less = filled
 
         @pl.when(full)
         def _():
-            order[0, n_full] = local
+            info[n_full, ORDER] = local
 
         @pl.when(jnp.logical_not(full))
         def _():
-            order[1, n_less] = local
+            info[n_less, ORDER + 1] = local
 
         step = full.astype(jnp.int32)
         return n_full + step, n_less + 1 - step
 
-    filled = lax.fori_loop(0, tiles, sort, (jnp.int32(0), jnp.int32(0)))
+    n_full, n_less = lax.fori_loop(0, tiles, sort, (jnp.int32(0), jnp.int32(0)))
+    info[0, FILLED] = n_full
+    info[0, FILLED + 1] = n_less
+
+
+def attend_kernel(own, sib, base_totals, base_peaks, info, outs, scores, peaks, totals, *, sources):
+    chips, tokens, _ = outs.shape
+    tile_len = sources * tokens
+    factor = math.log2(math.e) / math.sqrt(HEAD_DIM)
 
     def listed(local, m, part):
-        return rows_of(kv, place[local, m], sources, part, tokens)
+        place = info[local, m]
+        beside = place >= chips
+        first = jnp.where(beside, place - chips, place)
+        here = rows_of(own, first, sources, part, tokens)
+        there = rows_of(sib, first, sources, part, tokens)
+        return jnp.where(beside, there, here)
 
     def query_of(local):
         return rows_of(own, local * sources, sources, 2, tokens)
@@ -151,10 +152,10 @@
         totals[...] = total
 
     for kind, count in enumerate((MAXK, MAXK - 1)):
-        number = filled[kind]
+        number = info[0, FILLED + kind]
 
         def pick(i, kind=kind, number=number):
-            return order[kind, jnp.minimum(i, number - 1)]
+            return info[jnp.minimum(i, number - 1), ORDER + kind]
 
         def first(count=count, pick=pick):
             local = pick(0)
@@ -173,17 +174,25 @@
         pl.when(number > 0)(lambda pick=pick, number=number: finish(pick(number - 1)))
 
 
-def self_call(own, *, tokens, sources):
-    tiles, tile_len = own.shape[0] // sources, sources * tokens
+def self_call(own, *, row_len, row_tiles):
+    chips, tokens = own.shape[0], (own.shape[1] - TABLE_ROWS) // 3
+    sources = row_len // row_tiles
+    tiles, tile_len = chips // sources, sources * tokens
     flops = 4 * tiles * tile_len * tile_len * HEAD_DIM
     vmem = pl.BlockSpec(memory_space=pltpu.VMEM)
     return pl.pallas_call(
-        functools.partial(self_kernel, sources=sources, tokens=tokens),
+        functools.partial(self_kernel, row_len=row_len, row_tiles=row_tiles),
         in_specs=[vmem],
-        out_specs=[vmem, vmem],
+        out_specs=[vmem, vmem, pl.BlockSpec(memory_space=pltpu.SMEM)],
+        scratch_shapes=[
+            pltpu.VMEM((chips // row_len, 8, HEAD_DIM), jnp.int32),
+            pltpu.SMEM((chips // row_len, 8, HEAD_DIM), jnp.int32),
+            pltpu.SemaphoreType.DMA((1,)),
+        ],
         out_shape=[
             jax.ShapeDtypeStruct((tiles, tile_len, 2 * HEAD_DIM), jnp.float32),
             jax.ShapeDtypeStruct((tiles, tile_len, HEAD_DIM), jnp.float32),
+            jax.ShapeDtypeStruct((tiles, FILLED + 2), jnp.int32),
         ],
         compiler_params=pltpu.CompilerParams(vmem_limit_bytes=24 * MIB),
         cost_estimate=pl.CostEstimate(
@@ -193,26 +202,19 @@
     )(own)
 
 
-def attend_call(own, sib, totals, peaks, *, row_len, row_tiles):
+def attend_call(own, sib, totals, peaks, info, *, sources):
     chips, tokens = own.shape[0], sib.shape[1] // 2
-    sources = row_len // row_tiles
     tiles, tile_len, _ = peaks.shape
     flops = 4 * tiles * tile_len * (MAXK - 1) * tile_len * HEAD_DIM
     vmem = pl.BlockSpec(memory_space=pltpu.VMEM)
     return pl.pallas_call(
-        functools.partial(attend_kernel, row_len=row_len, row_tiles=row_tiles),
-        in_specs=[vmem] * 4,
+        functools.partial(attend_kernel, sources=sources),
+        in_specs=[vmem] * 4 + [pl.BlockSpec(memory_space=pltpu.SMEM)],
         out_specs=vmem,
         scratch_shapes=[
-            pltpu.VMEM((CORES * chips, 2 * tokens, HEAD_DIM), jnp.bfloat16),
             pltpu.VMEM((MAXK - 1, tile_len, tile_len), jnp.float32),
             pltpu.VMEM((tile_len, HEAD_DIM), jnp.float32),
             pltpu.VMEM((tile_len, 2 * HEAD_DIM), jnp.float32),
-            pltpu.VMEM((chips // row_len, 8, HEAD_DIM), jnp.int32),
-            pltpu.SMEM((chips // row_len, 8, HEAD_DIM), jnp.int32),
-            pltpu.SMEM((tiles, MAXK), jnp.int32),
-            pltpu.SMEM((2, tiles), jnp.int32),
-            pltpu.SemaphoreType.DMA((1,)),
         ],
         out_shape=jax.ShapeDtypeStruct((chips, tokens, HEAD_DIM), jnp.bfloat16),
         compiler_params=pltpu.CompilerParams(vmem_limit_bytes=24 * MIB),
@@ -220,7 +222,7 @@
             flops=flops, bytes_accessed=12 * MIB, transcendentals=flops // (4 * HEAD_DIM)
         ),
         name="attend",
-    )(own, sib, totals, peaks)
+    )(own, sib, totals, peaks, info)
 
 
 def local(queries, keys, values, pairs, pair_count):
@@ -257,8 +259,8 @@
     )
     swap = [(s, s ^ 1) for s in range(rows_all)]
     sib = lax.ppermute(own[:, : 2 * tokens], "seq", swap)
-    totals, peaks = self_call(own, tokens=tokens, sources=head_size // row_tiles)
-    attended = attend_call(own, sib, totals, peaks, row_len=head_size, row_tiles=row_tiles)
+    totals, peaks, info = self_call(own, row_len=head_size, row_tiles=row_tiles)
+    attended = attend_call(own, sib, totals, peaks, info, sources=head_size // row_tiles)
     back = lax.all_to_all(
         attended, axes, split_axis=0, concat_axis=0, tiled=True, axis_index_groups=same_core
     )

time: 128 us -> 126 us (0.984)
  Pallas kernels: 23.6 us -> 21.6 us
    pallas_call x2, Pallas kernels: 20.3 us -> 18.3 us  [the longest x1 12.5 us: attend_call(): pl.pallas_call(functools.partial(attend_kernel, sources=sources), in_spec...]
where the time goes in v8:
time: 126 us
  blocking collectives  99.9 us (79%)
  Pallas kernels  21.6 us (17%)
  starting transfers between devices  2.59 us (2%)
  local copies, waits for them, and re-layouts  1.44 us (1%)
    all_to_all x1, blocking collectives, local(): lax.all_to_all(packed, axes, split_axis=0, concat_axis=0, tiled=True, axi...  71.3 us
    all_to_all x1, blocking collectives, local(): lax.all_to_all(attended, axes, split_axis=0, concat_axis=0, tiled=True, a...  28.6 us
    pallas_call x1, Pallas kernels, attend_call(): pl.pallas_call(functools.partial(attend_kernel, sources=sources), in_spec...  12.5 us
    pallas_call x1, Pallas kernels, self_call(): pl.pallas_call(functools.partial(self_kernel, row_len=row_len, row_tiles=...  5.77 us
    pallas_call x1, Pallas kernels, local(): pl.pallas_call(pack_kernel, grid=(PACK_STEPS,), in_specs=[pl.BlockSpec((t...  3.25 us
    ppermute x1, starting transfers between devices, local(): sib = lax.ppermute(own[:, :2 * tokens], 'seq', swap)  2.59 us
  transfers between devices with their start and end apart: 1, of which 0 were waited for; matrix products, arithmetic and copies ran while one was open for 0% of the time, Pallas kernels for 5%

profile of v8, /device:TPU:1, one launch (start us, length us, event | category | flops | bytes accessed | tf_op | source)
XLA Modules:
  0.0 125.5 jit_solution(470483447296513492)
XLA Ops:
  0.0 3.2 %pack.1 = bf16[64,304,128]{2,1,0:T(8,128)(2,1)} custom-call(bf16[96,5120]{1,0:T(8,128)(2,1)} %q_ref.1, bf16[96,5120]{1,0:T(8,128)(2,1)} %k_ref.1, bf16[96,5120]{1,0:T(8,128)(2,1)} %v_ref.1, s32[2,4]{1,0:T(2,128)} %pairs_ref.1, s32[1,2]{1,0:T(1,128)} %bitcast.7), custom_call_target="tpu_custom_call" | custom-call | tf_op jit(solution)/shard_map/pack/pallas_call | solution.py:243
  3.3 71.3 %all_to_all.10.own = bf16[64,304,128]{2,1,0:T(8,128)(2,1)S(1)} all-to-all(bf16[64,304,128]{2,1,0:T(8,128)(2,1)} %pack.1), channel_id=1, replica_groups={{0,1,2,3,4,5,6,7,16,17,18,19,20,21,22,23,32,33,34,35,36,37,38,39,48,49,..., dimensions={0} | all-to-all | bytes 9961472 | tf_op jit(solution)/shard_map/all_to_all | solution.py:257
  74.5 0.4 slice.8
  74.9 2.6 %collective-permute-start = (bf16[64,192,128]{2,1,0:T(8,128)(2,1)S(1)}, bf16[64,192,128]{2,1,0:T(8,128)(2,1)S(1)}, u32[]{:S(2)}, u32[]{:S(2)}) collective-permute-start(bf16[64,192,128]{2,1,0:T(8,128)(2,1)S(1)} %slice.8), channel_id=1, source_target_pairs={{0,8},{8,0},{16,24},{24,16},{32,40},{40,32},{48,56},{56,48},{64,72... | collective-permute-start | bytes 9437192 | tf_op jit(solution)/shard_map/ppermute | solution.py:261
  77.5 5.8 %attend_self.1 = (f32[16,384,256]{2,1,0:T(8,128)S(1)}, f32[16,384,128]{2,1,0:T(8,128)S(1)}, s32[16,8]{1,0:T(8,128)S(1)}) custom-call(bf16[64,304,128]{2,1,0:T(8,128)(2,1)S(1)} %all_to_all.10.own), custom_call_target="tpu_custom_call" | custom-call | flops 1207959552 | bytes 12582912 | tf_op jit(solution)/shard_map/attend_self/pallas_call | solution.py:183
  83.3 0.0 collective-permute-done.sib
  83.3 12.5 %attend.1 = bf16[64,96,128]{2,1,0:T(8,128)(2,1)S(1)} custom-call(bf16[64,304,128]{2,1,0:T(8,128)(2,1)S(1)} %all_to_all.10.own, bf16[64,192,128]{2,1,0:T(8,128)(2,1)S(1)} %collective-permute-done.sib, f32[16,384,256]{2,1,0:T(8,128)S(1)} %get-tuple-element.8.base_totals, f32[16,384,128]{2,1,0:T(8,128)S(1)} %get-tuple-element.9.base_peaks, ...), custom_call_target="tpu_custom_call" | custom-call | flops 3623878656 | bytes 12582912 | tf_op jit(solution)/shard_map/attend/pallas_call | solution.py:210
  95.8 28.6 %all_to_all.11 = bf16[64,96,128]{2,1,0:T(8,128)(2,1)S(1)} all-to-all(bf16[64,96,128]{2,1,0:T(8,128)(2,1)S(1)} %attend.1), channel_id=1, replica_groups={{0,1,2,3,4,5,6,7,16,17,18,19,20,21,22,23,32,33,34,35,36,37,38,39,48,49,..., dimensions={0} | all-to-all | bytes 3145728 | tf_op jit(solution)/shard_map/all_to_all | solution.py:264
  124.5 1.0 copy_bitcast_fusion
Async XLA Ops:
  74.9 8.4 %collective-permute-start = (bf16[64,192,128]{2,1,0:T(8,128)(2,1)S(1)}, bf16[64,192,128]{2,1,0:T(8,128)(2,1)S(1)}, u32[]{:S(2)}, u32[]{:S(2)}) collective-permute-start(bf16[64,192,128]{2,1,0:T(8,128)(2,1)S(1)} %slice.8), channel_id=1, source_target_pairs={{0,8},{8,0},{16,24},{24,16},{32,40},{40,32},{48,56},{56,48},{64,72... | collective-permute-start | bytes 9437192 | tf_op jit(solution)/shard_map/ppermute | solution.py:261

commit v9 on v8

--- a/solution.py
+++ b/solution.py
@@ -87,14 +87,8 @@
         full = table[at, row_tiles, w] > MAXK - 1
         n_full, n_less = filled
 
-        @pl.when(full)
-        def _():
-            info[n_full, ORDER] = local
-
-        @pl.when(jnp.logical_not(full))
-        def _():
-            info[n_less, ORDER + 1] = local
-
+        info[n_full, ORDER] = local
+        info[n_less, ORDER + 1] = local
         step = full.astype(jnp.int32)
         return n_full + step, n_less + 1 - step
 

time: 126 us -> 125 us (level)
  no operation moved by 1% of the time
where the time goes in v9:
time: 125 us; the launch traced here: 124 us
  blocking collectives  98.7 us (79%)
  Pallas kernels  21.4 us (17%)
  starting transfers between devices  2.59 us (2%)
  local copies, waits for them, and re-layouts  1.44 us (1%)
    all_to_all x1, blocking collectives, local(): lax.all_to_all(packed, axes, split_axis=0, concat_axis=0, tiled=True, axi...  71.3 us
    all_to_all x1, blocking collectives, local(): lax.all_to_all(attended, axes, split_axis=0, concat_axis=0, tiled=True, a...  27.4 us
    pallas_call x1, Pallas kernels, attend_call(): pl.pallas_call(functools.partial(attend_kernel, sources=sources), in_spec...  12.4 us
    pallas_call x1, Pallas kernels, self_call(): pl.pallas_call(functools.partial(self_kernel, row_len=row_len, row_tiles=...  5.77 us
    pallas_call x1, Pallas kernels, local(): pl.pallas_call(pack_kernel, grid=(PACK_STEPS,), in_specs=[pl.BlockSpec((t...  3.25 us
    ppermute x1, starting transfers between devices, local(): sib = lax.ppermute(own[:, :2 * tokens], 'seq', swap)  2.59 us
  transfers between devices with their start and end apart: 1, of which 0 were waited for; matrix products, arithmetic and copies ran while one was open for 0% of the time, Pallas kernels for 5%

profile of v9, /device:TPU:1, one launch (start us, length us, event | category | flops | bytes accessed | tf_op | source)
XLA Modules:
  0.0 124.1 jit_solution(5576934688639350260)
XLA Ops:
  0.0 3.2 %pack.1 = bf16[64,304,128]{2,1,0:T(8,128)(2,1)} custom-call(bf16[96,5120]{1,0:T(8,128)(2,1)} %q_ref.1, bf16[96,5120]{1,0:T(8,128)(2,1)} %k_ref.1, bf16[96,5120]{1,0:T(8,128)(2,1)} %v_ref.1, s32[2,4]{1,0:T(2,128)} %pairs_ref.1, s32[1,2]{1,0:T(1,128)} %bitcast.7), custom_call_target="tpu_custom_call" | custom-call | tf_op jit(solution)/shard_map/pack/pallas_call | solution.py:237
  3.3 71.3 %all_to_all.10.own = bf16[64,304,128]{2,1,0:T(8,128)(2,1)S(1)} all-to-all(bf16[64,304,128]{2,1,0:T(8,128)(2,1)} %pack.1), channel_id=1, replica_groups={{0,1,2,3,4,5,6,7,16,17,18,19,20,21,22,23,32,33,34,35,36,37,38,39,48,49,..., dimensions={0} | all-to-all | bytes 9961472 | tf_op jit(solution)/shard_map/all_to_all | solution.py:251
  74.5 0.4 slice.8
  74.9 2.6 %collective-permute-start = (bf16[64,192,128]{2,1,0:T(8,128)(2,1)S(1)}, bf16[64,192,128]{2,1,0:T(8,128)(2,1)S(1)}, u32[]{:S(2)}, u32[]{:S(2)}) collective-permute-start(bf16[64,192,128]{2,1,0:T(8,128)(2,1)S(1)} %slice.8), channel_id=1, source_target_pairs={{0,8},{8,0},{16,24},{24,16},{32,40},{40,32},{48,56},{56,48},{64,72... | collective-permute-start | bytes 9437192 | tf_op jit(solution)/shard_map/ppermute | solution.py:255
  77.5 5.8 %attend_self.1 = (f32[16,384,256]{2,1,0:T(8,128)S(1)}, f32[16,384,128]{2,1,0:T(8,128)S(1)}, s32[16,8]{1,0:T(8,128)S(1)}) custom-call(bf16[64,304,128]{2,1,0:T(8,128)(2,1)S(1)} %all_to_all.10.own), custom_call_target="tpu_custom_call" | custom-call | flops 1207959552 | bytes 12582912 | tf_op jit(solution)/shard_map/attend_self/pallas_call | solution.py:177
  83.3 0.0 collective-permute-done.sib
  83.3 12.4 %attend.1 = bf16[64,96,128]{2,1,0:T(8,128)(2,1)S(1)} custom-call(bf16[64,304,128]{2,1,0:T(8,128)(2,1)S(1)} %all_to_all.10.own, bf16[64,192,128]{2,1,0:T(8,128)(2,1)S(1)} %collective-permute-done.sib, f32[16,384,256]{2,1,0:T(8,128)S(1)} %get-tuple-element.8.base_totals, f32[16,384,128]{2,1,0:T(8,128)S(1)} %get-tuple-element.9.base_peaks, ...), custom_call_target="tpu_custom_call" | custom-call | flops 3623878656 | bytes 12582912 | tf_op jit(solution)/shard_map/attend/pallas_call | solution.py:204
  95.7 27.4 %all_to_all.11 = bf16[64,96,128]{2,1,0:T(8,128)(2,1)S(1)} all-to-all(bf16[64,96,128]{2,1,0:T(8,128)(2,1)S(1)} %attend.1), channel_id=1, replica_groups={{0,1,2,3,4,5,6,7,16,17,18,19,20,21,22,23,32,33,34,35,36,37,38,39,48,49,..., dimensions={0} | all-to-all | bytes 3145728 | tf_op jit(solution)/shard_map/all_to_all | solution.py:258
  123.1 1.0 copy_bitcast_fusion
Async XLA Ops:
  74.9 8.4 %collective-permute-start = (bf16[64,192,128]{2,1,0:T(8,128)(2,1)S(1)}, bf16[64,192,128]{2,1,0:T(8,128)(2,1)S(1)}, u32[]{:S(2)}, u32[]{:S(2)}) collective-permute-start(bf16[64,192,128]{2,1,0:T(8,128)(2,1)S(1)} %slice.8), channel_id=1, source_target_pairs={{0,8},{8,0},{16,24},{24,16},{32,40},{40,32},{48,56},{56,48},{64,72... | collective-permute-start | bytes 9437192 | tf_op jit(solution)/shard_map/ppermute | solution.py:255
